TPU v7x, 32 devices: a whole 2x2x4 slice. The times are simulated.
32 devices in a mesh: wide: 8 (over y, x, core), narrow: 4 (over z).
Axes of the slice: x: 2, y: 2, z: 4, core: 2. Of those that a mesh axis runs over, the one named last changes fastest.
Arguments:
- inputs: bfloat16 [10240, 768], P(('wide', 'narrow')), may hold values from -6 to 6
- pass_ids: int32 [8, 1280], P('wide'), may hold values from 0 to 4, as said below
- front_gain: bfloat16 [768], replicated, may hold values from 0.25 to 1.75
- front_shift: bfloat16 [768], replicated, may hold values from -3 to 3
- triple_weight: bfloat16 [3, 768, 768], P(None, None, 'narrow'), may hold values from -0.21875 to 0.21875
- triple_bias: bfloat16 [2, 768], P(None, 'narrow'), may hold values from -3 to 3
- mixer_weight: bfloat16 [768, 768], replicated, may hold values from -0.875 to 0.875
- mixer_bias: bfloat16 [768], replicated, may hold values from -3 to 3
- back_gain: bfloat16 [768], replicated, may hold values from 0.25 to 1.75
- back_shift: bfloat16 [768], replicated, may hold values from -3 to 3
- expand_weight: bfloat16 [768, 3072], replicated, may hold values from -0.21875 to 0.21875
- expand_bias: bfloat16 [3072], replicated, may hold values from -3 to 3
- reduce_weight: bfloat16 [3072, 768], replicated, may hold values from -0.109375 to 0.109375
- reduce_bias: bfloat16 [768], replicated, may hold values from -3 to 3
- pass_table: bfloat16 [5, 768], replicated, may hold values from -3 to 3
- cotangent: bfloat16 [10240, 768], P(('wide', 'narrow')), may hold values from -15 to 15
Outputs:
- layer_out: bfloat16 [10240, 768], P(('wide', 'narrow'))
- grad_inputs: bfloat16 [10240, 768], P(('wide', 'narrow'))
- grad_front_gain: float32 [768], replicated
- grad_front_shift: float32 [768], replicated
- grad_triple_weight: float32 [3, 768, 768], P(None, None, 'narrow')
- grad_triple_bias: float32 [2, 768], P(None, 'narrow')
- grad_mixer_weight: float32 [768, 768], P('wide', 'narrow')
- grad_mixer_bias: float32 [768], replicated
- grad_back_gain: float32 [768], replicated
- grad_back_shift: float32 [768], replicated
- grad_expand_weight: float32 [768, 3072], P('wide', 'narrow')
- grad_expand_bias: float32 [3072], replicated
- grad_reduce_weight: float32 [3072, 768], P('wide', 'narrow')
- grad_reduce_bias: float32 [768], replicated
- grad_pass_table: float32 [5, 768], replicated
Inputs may be any that keep to these rules, and one draw needn't show every extreme that they name: `pass_ids`: in each sequence the first 5 rows are passes 0 to 4 of its first token; every later row has pass 0 or one more than the row before it.
All inputs are finite; a program needn't handle non-finite values.
Results may differ from a plain program's by a relative error of at most 0.013.
Values may be sent and summed in bfloat16 or wider, within the bound.
No kernel may reach another device: no remote copies, remote signals or barrier semaphores. Data moves between devices by JAX's collectives and lax.ppermute only.
A program may use at most 128 MiB of HBM per device.

v0:
```python
import math

import jax
import jax.numpy as jnp
from jax import lax
from jax.experimental import pallas as pl
from jax.experimental.pallas import tpu as pltpu
from jax.sharding import PartitionSpec as P


HEAD_DIM = 64
EPSILON = 1e-05
BLOCK = 256
LONG_FORWARD, LONG_BACKWARD = 768, 1280
HIDDEN = -1e30
F32 = jnp.float32
BF16 = jnp.bfloat16
MIB = 1024 * 1024
AXES = ("wide", "narrow")
NN = (((1,), (0,)), ((), ()))
NT = (((1,), (1,)), ((), ()))
TN = (((0,), (0,)), ((), ()))
GELU_A = math.sqrt(2.0 / math.pi)
GELU_B = 0.044715
shape = jax.ShapeDtypeStruct

FRONT_GAIN, FRONT_SHIFT, MIXER_BIAS, BACK_GAIN, BACK_SHIFT, REDUCE_BIAS, EXPAND_BIAS, TABLE = 0, 1, 2, 3, 4, 5, 6, 10
SUM_TABLE, SUM_COT, SUM_MIXER, SUM_GAIN, SUM_SHIFT, SUM_EXPAND = 0, 5, 6, 7, 8, 9
SUM_FRONT_GAIN, SUM_FRONT_SHIFT, SUM_TRIPLE = 16, 17, 18
SUMS = 24


def dot(left, right, dims=NN):
    return lax.dot_general(left, right, dims, preferred_element_type=F32)


def whole():
    return pl.BlockSpec(memory_space=pltpu.VMEM)


def call(kernel, outs, *arrays, scratch=(), vmem=12, name=None):
    return pl.pallas_call(
        kernel,
        out_shape=tuple(outs),
        in_specs=[pl.BlockSpec(memory_space=pltpu.SMEM)] + [whole()] * (len(arrays) - 1),
        out_specs=(whole(),) * len(outs),
        scratch_shapes=list(scratch),
        compiler_params=pltpu.CompilerParams(vmem_limit_bytes=vmem * MIB),
        name=name,
    )(*arrays)


def unit_rows(values):
    centred = values - jnp.mean(values, axis=-1, keepdims=True)
    scale = lax.rsqrt(jnp.mean(centred * centred, axis=-1, keepdims=True) + EPSILON)
    return centred * scale, scale


def norm_pullback(grad_out, unit, scale, gain):
    grad_unit = grad_out * gain
    inner = (
        grad_unit
        - jnp.mean(grad_unit, axis=-1, keepdims=True)
        - unit * jnp.mean(grad_unit * unit, axis=-1, keepdims=True)
    )
    return inner * scale


def column_sum(values):
    return jnp.sum(values, axis=0, keepdims=True)


def put_sums(packet_ref, start, sums):
    high = sums.astype(BF16)
    packet_ref[start : start + SUMS, :] = high
    packet_ref[start + SUMS : start + 2 * SUMS, :] = (sums - high.astype(F32)).astype(BF16)


def get_sums(packet_ref, start):
    return packet_ref[start : start + SUMS, :].astype(F32) + packet_ref[start + SUMS : start + 2 * SUMS, :].astype(F32)


def keep_head(block, head, axis):
    place = lax.broadcasted_iota(jnp.int32, block.shape, axis) // HEAD_DIM
    return jnp.where(place == head, block, jnp.zeros_like(block))


def rows_at(index, count):
    if isinstance(index, int):
        return slice(index * count, (index + 1) * count)
    return pl.ds(pl.multiple_of(index * count, math.gcd(count, 64)), count)


def each_head(heads, one_head, looped):
    if looped:
        lax.fori_loop(0, heads, lambda head, carry: one_head(head) or carry, 0)
    else:
        for head in range(heads):
            one_head(head)


def vector(vectors_ref, index):
    return vectors_ref[index : index + 1, :]


def pass_ids_of(tail_ref, row_ref, col_ref):
    width = tail_ref.shape[1]
    rows = row_ref.shape[1]
    tail = tail_ref[...].astype(F32)
    row_ref[:, 0:width] = tail[1:2, :]
    row_ref[:, width:rows] = tail[2:3, 0 : rows - width]
    for start in range(0, rows, BLOCK):
        col_ref[start : start + BLOCK, :] = jnp.broadcast_to(row_ref[:, start : start + BLOCK], (128, BLOCK)).T


def visibility(ids_col_ref, ids_row_ref, start, keys):
    seen = ids_col_ref[0:keys, 0:1] <= ids_row_ref[:, start : start + BLOCK]
    key_place = lax.broadcasted_iota(jnp.int32, (keys, BLOCK), 0)
    query_place = lax.broadcasted_iota(jnp.int32, (keys, BLOCK), 1) + start
    return jnp.where(seen & (key_place <= query_place), 0.0, HIDDEN).astype(F32)


def vectors_kernel(place_ref, bias_ref, ids_ref, *refs):
    tail_ref, out_ref, table_ref, long_ref = refs[-1], refs[-2], refs[-3], refs[-4]
    width = out_ref.shape[1]
    out_ref[...] = jnp.zeros_like(out_ref)
    for index, ref in enumerate(refs[:-4]):
        out_ref[index : index + 1, :] = ref[...].astype(F32).reshape(1, width)
    for index in range(long_ref.shape[0] // width):
        part = long_ref[index * width : (index + 1) * width]
        out_ref[EXPAND_BIAS + index : EXPAND_BIAS + index + 1, :] = part.astype(F32).reshape(1, width)
    out_ref[TABLE : TABLE + table_ref.shape[0], :] = table_ref[...].astype(F32)
    ids = ids_ref[...].astype(F32)
    bias = bias_ref[...].astype(F32)
    rest, double = ids.shape[1] - width, 2 * bias.shape[1]
    tail = [
        jnp.concatenate([bias[0:1, :], bias[1:2, :], jnp.zeros((1, width - double), F32)], axis=1),
        ids[:, 0:width],
        jnp.concatenate([ids[:, width:], jnp.zeros((1, width - rest), F32)], axis=1),
        jnp.zeros((13, width), F32),
    ]
    tail_ref[...] = jnp.concatenate(tail, axis=0).astype(BF16)


def gather_vectors(place, bias, ids, *arrays):
    width = arrays[0].shape[0]
    return call(
        vectors_kernel,
        [shape((16, width), F32), shape((16, width), BF16)],
        place, bias, ids, *arrays,
        vmem=4,
        name="gather_vectors",
    )


def attend_forward_kernel(
    place_ref, x0_ref, x1_ref, x2_ref, x3_ref, tail_ref, vectors_ref, weight_own_ref, p0_ref, p1_ref, p2_ref, p3_ref,
    m0_ref, m1_ref, m2_ref, m3_ref, mixed_t_ref, normed_ref, triple_ref, weight_ref,
    ids_row_ref, ids_col_ref, q_t_ref, v_t_ref, bias_t_ref, mixed_ref, straight_ref,
):
    me, stay, corner = place_ref[0], place_ref[5], place_ref[7]
    _, rows, part = triple_ref.shape
    local = x0_ref.shape[0]
    piece = p0_ref.shape[0]
    heads = part // HEAD_DIM
    gain = vector(vectors_ref, FRONT_GAIN)
    shift = vector(vectors_ref, FRONT_SHIFT)
    pass_ids_of(tail_ref, ids_row_ref, ids_col_ref)

    @pl.when(stay == 1)
    def _():
        weight_ref[...] = weight_own_ref[...]

    @pl.when(stay == 0)
    def _():
        for slot, value in enumerate((p0_ref, p1_ref, p2_ref, p3_ref)):
            weight_ref[rows_at(corner ^ slot, piece), :] = value[...]

    straight_ref[...] = weight_ref[...].T
    bias = tail_ref[0:1, 0 : 2 * part].astype(F32)
    for slot, x_ref in enumerate((x0_ref, x1_ref, x2_ref, x3_ref)):
        here = rows_at(me ^ slot, local)
        unit, _ = unit_rows(x_ref[...].astype(F32))
        normed = (unit * gain + shift).astype(BF16)
        normed_ref[here, :] = normed
        q = (dot(normed, straight_ref[:, 0:part]) + bias[:, 0:part]).astype(BF16)
        triple_ref[0, here, :] = q * jnp.asarray(HEAD_DIM**-0.5, BF16)
        triple_ref[1, here, :] = dot(normed, straight_ref[:, part : 2 * part]).astype(BF16)
        triple_ref[2, here, :] = (dot(normed, straight_ref[:, 2 * part : 3 * part]) + bias[:, part : 2 * part]).astype(BF16)

    for start in range(0, rows, BLOCK):
        cols = slice(start, start + BLOCK)
        q_t_ref[:, cols] = triple_ref[0, cols, :].T
        v_t_ref[:, cols] = triple_ref[2, cols, :].T

    mixed_t_ref[part : part + 8, :] = jnp.zeros((8, rows), F32)
    for start in range(0, rows, BLOCK):
        keys = start + BLOCK
        cols = slice(start, keys)
        bias_t_ref[0:keys, :] = visibility(ids_col_ref, ids_row_ref, start, keys)

        def one_head(head, keys=keys, cols=cols):
            here = rows_at(head, HEAD_DIM)
            scores = dot(triple_ref[1, 0:keys, :], keep_head(q_t_ref[:, cols], head, 0)) + bias_t_ref[0:keys, :]
            top = jnp.max(scores, axis=0, keepdims=True)
            weights = jnp.exp(scores - top)
            total = jnp.sum(weights, axis=0, keepdims=True)
            mixed_t_ref[here, cols] = dot(v_t_ref[here, 0:keys], weights.astype(BF16)) / total
            mixed_t_ref[pl.ds(part + head, 1), cols] = top + jnp.log(total)

        each_head(heads, one_head, keys > LONG_FORWARD)
        mixed_ref[cols, :] = mixed_t_ref[0:part, cols].T.astype(BF16)
    for slot, out_ref in enumerate((m0_ref, m1_ref, m2_ref, m3_ref)):
        pack_rows(out_ref, mixed_ref, me ^ slot)


def pack_rows(out_ref, rows_ref, index):
    half, part = out_ref.shape[0], out_ref.shape[1] // 2
    out_ref[:, 0:part] = rows_ref[rows_at(2 * index, half), :]
    out_ref[:, part : 2 * part] = rows_ref[rows_at(2 * index + 1, half), :]


def unpack_rows(rows_ref, packed_ref, index):
    half, part = packed_ref.shape[0], packed_ref.shape[1] // 2
    rows_ref[rows_at(2 * index, half), :] = packed_ref[:, 0:part]
    rows_ref[rows_at(2 * index + 1, half), :] = packed_ref[:, part : 2 * part]


def attend_forward(place, shards, tail, vectors, weight, pieces):
    local, width = shards[0].shape
    rows = 4 * local
    part = weight.shape[0] // 3
    return call(
        attend_forward_kernel,
        [shape((local // 2, 2 * part), BF16)] * 4
        + [
            shape((part + 8, rows), F32),
            shape((rows, width), BF16),
            shape((3, rows, part), BF16),
            shape(weight.shape, BF16),
        ],
        place, *shards, tail, vectors, weight, *pieces,
        scratch=[
            pltpu.VMEM((1, rows), F32),
            pltpu.VMEM((rows, 128), F32),
            pltpu.VMEM((part, rows), BF16),
            pltpu.VMEM((part, rows), BF16),
            pltpu.VMEM((rows, BLOCK), F32),
            pltpu.VMEM((rows, part), BF16),
            pltpu.VMEM((width, 3 * part), BF16),
        ],
        vmem=16,
        name="attend_forward",
    )


def attend_backward_kernel(
    place_ref, g0_ref, g1_ref, g2_ref, g3_ref, triple_ref, mixed_t_ref, tail_ref, weight_ref,
    near_ref, far_ref, grad_triple_ref,
    grad_ref, grad_t_ref, delta_ref, grad_q_t_ref, grad_k_ref, grad_v_ref, bias_t_ref,
    ids_row_ref, ids_col_ref, q_t_ref, k_t_ref,
):
    me = place_ref[0]
    _, rows, part = triple_ref.shape
    local = near_ref.shape[1]
    heads = part // HEAD_DIM
    for slot, packed_ref in enumerate((g0_ref, g1_ref, g2_ref, g3_ref)):
        unpack_rows(grad_ref, packed_ref, me ^ slot)
    pass_ids_of(tail_ref, ids_row_ref, ids_col_ref)
    for start in range(0, rows, BLOCK):
        cols = slice(start, start + BLOCK)
        q_t_ref[:, cols] = triple_ref[0, cols, :].T
        k_t_ref[:, cols] = triple_ref[1, cols, :].T
        grad_t = grad_ref[cols, :].T
        grad_t_ref[:, cols] = grad_t
        product = grad_t.astype(F32) * mixed_t_ref[0:part, cols]
        for head in range(heads):
            delta_ref[head : head + 1, cols] = column_sum(product[head * HEAD_DIM : (head + 1) * HEAD_DIM, :])
    grad_k_ref[...] = jnp.zeros_like(grad_k_ref)
    grad_v_ref[...] = jnp.zeros_like(grad_v_ref)
    for start in range(0, rows, BLOCK):
        keys = start + BLOCK
        cols = slice(start, keys)
        bias_t_ref[0:keys, :] = visibility(ids_col_ref, ids_row_ref, start, keys)

        def one_head(head, keys=keys, cols=cols):
            here = rows_at(head, HEAD_DIM)
            scores = dot(triple_ref[1, 0:keys, :], keep_head(q_t_ref[:, cols], head, 0))
            probs = jnp.exp(scores + bias_t_ref[0:keys, :] - mixed_t_ref[pl.ds(part + head, 1), cols])
            grad_probs = dot(triple_ref[2, 0:keys, :], keep_head(grad_t_ref[:, cols], head, 0))
            grad_scores = (probs * (grad_probs - delta_ref[pl.ds(head, 1), cols])).astype(BF16)
            grad_v_ref[0:keys, :] += dot(probs.astype(BF16), keep_head(grad_ref[cols, :], head, 1))
            grad_k_ref[0:keys, :] += dot(grad_scores, keep_head(triple_ref[0, cols, :], head, 1))
            grad_q_t_ref[here, cols] = dot(k_t_ref[here, 0:keys], grad_scores)

        each_head(heads, one_head, keys > LONG_BACKWARD)
    factor = HEAD_DIM**-0.5
    for start in range(0, rows, BLOCK):
        cols = slice(start, start + BLOCK)
        grad_triple_ref[0, cols, :] = (grad_q_t_ref[:, cols].T * factor).astype(BF16)
    grad_triple_ref[1] = grad_k_ref[...].astype(BF16)
    grad_triple_ref[2] = grad_v_ref[...].astype(BF16)
    for slot in range(4):
        here = rows_at(me ^ slot, local)
        target = near_ref if slot < 2 else far_ref
        target[slot % 2] = (
            dot(grad_triple_ref[0, here, :], weight_ref[0:part, :])
            + dot(grad_triple_ref[1, here, :], weight_ref[part : 2 * part, :])
            + dot(grad_triple_ref[2, here, :], weight_ref[2 * part : 3 * part, :])
        ).astype(BF16)


def attend_backward(place, grads, triple, mixed_t, tail, weight):
    _, rows, part = triple.shape
    width = weight.shape[1]
    heads = part // HEAD_DIM
    pair = shape((2, rows // 4, width), BF16)
    return call(
        attend_backward_kernel,
        [pair, pair, shape((3, rows, part), BF16)],
        place, *grads, triple, mixed_t, tail, weight,
        scratch=[
            pltpu.VMEM((rows, part), BF16),
            pltpu.VMEM((part, rows), BF16),
            pltpu.VMEM((heads, rows), F32),
            pltpu.VMEM((part, rows), F32),
            pltpu.VMEM((rows, part), F32),
            pltpu.VMEM((rows, part), F32),
            pltpu.VMEM((rows, BLOCK), F32),
            pltpu.VMEM((1, rows), F32),
            pltpu.VMEM((rows, 128), F32),
            pltpu.VMEM((part, rows), BF16),
            pltpu.VMEM((part, rows), BF16),
        ],
        vmem=16,
        name="attend_backward",
    )


def mixer_kernel(
    place_ref, m0_ref, m1_ref, m2_ref, m3_ref, x_ref, mixer_ref, vectors_ref, _later_ref,
    normed_ref, middle_ref, mixed_ref,
):
    me = place_ref[0]
    half, double = m0_ref.shape
    part = double // 2
    middle = x_ref[...].astype(F32) + vector(vectors_ref, MIXER_BIAS)
    for slot, packed_ref in enumerate((m0_ref, m1_ref, m2_ref, m3_ref)):
        cols = slice(slot * part, (slot + 1) * part)
        mixed_ref[0:half, cols] = packed_ref[:, 0:part]
        mixed_ref[half : 2 * half, cols] = packed_ref[:, part:double]
        middle += dot(mixed_ref[:, cols], mixer_ref[rows_at(me ^ slot, part), :])
    middle_ref[...] = middle
    unit, _ = unit_rows(middle)
    normed_ref[...] = (unit * vector(vectors_ref, BACK_GAIN) + vector(vectors_ref, BACK_SHIFT)).astype(BF16)


def mixer_part(place, packed, x, mixer, vectors, later):
    rows, width = x.shape
    return call(
        mixer_kernel,
        [shape((rows, width), BF16), shape((rows, width), F32), shape((rows, width), BF16)],
        place, *packed, x, mixer, vectors, later,
        name="mixer_part",
    )


def feed_kernel(
    place_ref, normed_own_ref, normed_other_ref, cot_own_ref, cot_other_ref, expand_ref, reduce_ref, vectors_ref,
    second_ref, grad_ref, send_ref, active_ref, grad_hidden_ref, bias_sum_ref,
    total_ref, back_ref,
):
    side = place_ref[1]
    rows = normed_own_ref.shape[0]
    chunk = active_ref.shape[1] // 4
    lane = lax.broadcasted_iota(jnp.int32, (1, 2 * chunk), 1) // chunk
    total_ref[...] = jnp.zeros_like(total_ref)
    back_ref[...] = jnp.zeros_like(back_ref)

    def one_chunk(index, carry):
        block = pl.ds(pl.multiple_of((2 * index + side) * chunk, 128), chunk)
        expand = expand_ref[:, block]
        reduce = reduce_ref[block, :]
        bias = vectors_ref[pl.ds(EXPAND_BIAS + index, 1), pl.ds(pl.multiple_of(side * chunk, 128), chunk)]
        sums = jnp.zeros((1, chunk), F32)
        for part, (normed_ref, cot_ref) in enumerate(((normed_own_ref, cot_own_ref), (normed_other_ref, cot_other_ref))):
            here = slice(part * rows, (part + 1) * rows)
            cols = pl.ds(pl.multiple_of(index * chunk, 128), chunk)
            hidden = dot(normed_ref[...], expand) + bias
            square = hidden * hidden
            bend = jnp.tanh(GELU_A * hidden * (1.0 + GELU_B * square))
            half = 0.5 * (1.0 + bend)
            active = (hidden * half).astype(BF16)
            active_ref[here, cols] = active
            total_ref[here, :] += dot(active, reduce)
            slope = half + (0.5 * GELU_A) * hidden * (1.0 - bend * bend) * (1.0 + (3.0 * GELU_B) * square)
            grad_hidden = (dot(cot_ref[...], reduce, NT) * slope).astype(BF16)
            grad_hidden_ref[here, cols] = grad_hidden
            sums += column_sum(grad_hidden.astype(F32))
            back_ref[here, :] += dot(grad_hidden, expand, NT)
        bias_sum_ref[pl.ds(index, 1), :] = jnp.where(lane == side, jnp.concatenate([sums, sums], axis=1), 0.0)
        return carry

    lax.fori_loop(0, 4, one_chunk, 0)
    second_ref[...] = total_ref[0:rows, :]
    grad_ref[...] = back_ref[0:rows, :]
    send_ref[0] = back_ref[rows : 2 * rows, :].astype(BF16)
    send_ref[1] = total_ref[rows : 2 * rows, :].astype(BF16)


def feed_part(place, normed_own, normed_other, cot_own, cot_other, expand, reduce, vectors):
    rows, width = normed_own.shape
    hidden = expand.shape[1]
    return call(
        feed_kernel,
        [
            shape((rows, width), F32),
            shape((rows, width), F32),
            shape((2, rows, width), BF16),
            shape((2 * rows, hidden // 2), BF16),
            shape((2 * rows, hidden // 2), BF16),
            shape((4, width), F32),
        ],
        place, normed_own, normed_other, cot_own, cot_other, expand, reduce, vectors,
        scratch=[
            pltpu.VMEM((2 * rows, width), F32),
            pltpu.VMEM((2 * rows, width), F32),
        ],
        vmem=16,
        name="feed_part",
    )


def joint_kernel(
    place_ref, grad_own_ref, recv_ref, middle_ref, cot_ref, mixer_ref, vectors_ref,
    grad_middle_ref, grad_low_ref, g0_ref, g1_ref, g2_ref, g3_ref,
):
    me = place_ref[0]
    half, double = g0_ref.shape
    part = double // 2
    grad_normed = grad_own_ref[...] + recv_ref[0].astype(F32)
    unit, scale = unit_rows(middle_ref[...])
    back = norm_pullback(grad_normed, unit, scale, vector(vectors_ref, BACK_GAIN))
    grad_middle = cot_ref[...].astype(F32) + back
    grad_middle_ref[...] = grad_middle
    grad_low = grad_middle.astype(BF16)
    grad_low_ref[...] = grad_low
    for slot, packed_ref in enumerate((g0_ref, g1_ref, g2_ref, g3_ref)):
        grad = dot(grad_low, mixer_ref[rows_at(me ^ slot, part), :], NT).astype(BF16)
        packed_ref[:, 0:part] = grad[0:half, :]
        packed_ref[:, part:double] = grad[half : 2 * half, :]


def joint_part(place, *arrays):
    rows, width = arrays[0].shape
    part = width // 4
    return call(
        joint_kernel,
        [shape((rows, width), F32), shape((rows, width), BF16)] + [shape((rows // 2, 2 * part), BF16)] * 4,
        place, *arrays,
        name="joint_part",
    )


def outer_kernel(
    place_ref, second_ref, grad_own_ref, recv_ref, middle_ref, cot_ref, grad_low_ref, mixed_ref,
    tail_ref, vectors_ref, bias_sum_ref,
    out_ref, sums_ref, mixer_send_ref, mixer_keep_ref,
    total_ref, ids_row_ref, ids_ref,
):
    me, side = place_ref[0], place_ref[1]
    rows = cot_ref.shape[0]
    cot = cot_ref[...].astype(F32)
    unit, _ = unit_rows(middle_ref[...])
    pass_ids_of(tail_ref, ids_row_ref, ids_ref)
    grad_normed = grad_own_ref[...] + recv_ref[0].astype(F32)
    sums_ref[...] = jnp.zeros_like(sums_ref)
    passes = lax.broadcasted_iota(jnp.int32, (rows, 128), 1).astype(F32)
    chosen = (ids_ref[rows_at(me, rows), :] == passes).astype(BF16)
    table = vectors_ref[TABLE : TABLE + 5, :]
    embedded = dot(chosen, jnp.concatenate([table, jnp.zeros((123, table.shape[1]), F32)], axis=0).astype(BF16))
    sums_ref[SUM_TABLE : SUM_TABLE + 5, :] = dot(chosen, cot_ref[...], TN)[0:5, :]
    second = second_ref[...] + recv_ref[1].astype(F32) + vector(vectors_ref, REDUCE_BIAS)
    out_ref[...] = (middle_ref[...] + second + embedded).astype(BF16)
    sums_ref[SUM_COT : SUM_COT + 1, :] = column_sum(cot)
    sums_ref[SUM_MIXER : SUM_MIXER + 1, :] = column_sum(grad_low_ref[...].astype(F32))
    sums_ref[SUM_GAIN : SUM_GAIN + 1, :] = column_sum(grad_normed * unit)
    sums_ref[SUM_SHIFT : SUM_SHIFT + 1, :] = column_sum(grad_normed)
    sums_ref[SUM_EXPAND : SUM_EXPAND + 4, :] = bias_sum_ref[...]
    block = mixer_send_ref.shape[1]
    total_ref[...] = dot(mixed_ref[...], grad_low_ref[...], TN).astype(BF16)
    for slot in range(4):
        mixer_keep_ref[me ^ slot] = total_ref[rows_at(2 * slot + side, block), :]
        mixer_send_ref[me ^ slot] = total_ref[rows_at(2 * slot + (1 - side), block), :]


def outer_part(place, *arrays, seq_rows):
    rows, width = arrays[0].shape
    part = shape((4, width // 8, width), BF16)
    return call(
        outer_kernel,
        [shape((rows, width), BF16), shape((16, width), F32), part, part],
        place, *arrays,
        scratch=[pltpu.VMEM((width, width), BF16), pltpu.VMEM((1, seq_rows), F32), pltpu.VMEM((seq_rows, 128), F32)],
        name="outer_part",
    )


def flip(index):
    return ((index & 1) << 1) | (index >> 1)


def quarter_at(slot, quarter, side):
    return quarter ^ jnp.where(side == 0, flip(slot), slot)


def transposed_rows(out_ref, own_ref, other_ref, spare_ref, places):
    rows, width = own_ref.shape
    part = width // 4
    spare_ref[:, 0:rows] = own_ref[...].T
    spare_ref[:, rows : 2 * rows] = other_ref[...].T
    for index, place in enumerate(places):
        out_ref[index * part : (index + 1) * part, :] = spare_ref[rows_at(place, part), :]


def reduce_grads_kernel(place_ref, cot_own_ref, cot_other_ref, active_ref, send_ref, keep_ref, cot_t_ref, spare_ref):
    side, quarter, me_n = place_ref[1], place_ref[2], place_ref[3]
    chunk = active_ref.shape[1] // 4
    part = send_ref.shape[2]
    transposed_rows(cot_t_ref, cot_own_ref, cot_other_ref, spare_ref, [me_n ^ flip(index) for index in range(4)])
    for base, target in ((0, keep_ref), (2, send_ref)):

        def one_slot(step, carry, base=base, target=target):
            cols = pl.ds(pl.multiple_of(quarter_at(base + step, quarter, side) * chunk, 128), chunk)
            reduce = dot(cot_t_ref[...], active_ref[:, cols]).astype(BF16)
            for index in range(4):
                target[step, index] = reduce[index * part : (index + 1) * part, :]
            return carry

        lax.fori_loop(0, 2, one_slot, 0)


def reduce_grads(place, cot_own, cot_other, active):
    rows, width = cot_own.shape
    out = shape((2, 4, width // 4, active.shape[1] // 4), BF16)
    return call(
        reduce_grads_kernel,
        [out, out],
        place, cot_own, cot_other, active,
        scratch=[pltpu.VMEM((width, 2 * rows), BF16), pltpu.VMEM((width, 2 * rows), BF16)],
        name="reduce_grads",
    )


def expand_grads_kernel(
    place_ref, normed_own_ref, normed_other_ref, grad_hidden_ref, mixer_keep_ref, mixer_recv_ref,
    send_ref, keep_ref,
    normed_t_ref, spare_ref,
):
    side, quarter, me_n = place_ref[1], place_ref[2], place_ref[3]
    width = normed_own_ref.shape[1]
    chunk = grad_hidden_ref.shape[1] // 4
    high = width // 4
    quarters = [quarter_at(slot, quarter, side) for slot in range(4)]
    transposed_rows(normed_t_ref, normed_own_ref, normed_other_ref, spare_ref, quarters)

    def one_chunk(index, carry):
        cols = pl.ds(pl.multiple_of((me_n ^ flip(index)) * chunk, 128), chunk)
        expand = dot(normed_t_ref[...], grad_hidden_ref[:, cols]).astype(BF16)
        for slot in range(4):
            target = keep_ref if slot < 2 else send_ref
            target[slot % 2, index, 0:high, :] = expand[slot * high : (slot + 1) * high, :]
        return carry

    lax.fori_loop(0, 4, one_chunk, 0)
    for base, target in ((0, keep_ref), (2, send_ref)):

        def one_slot(step, carry, base=base, target=target):
            place = quarter_at(base + step, quarter, side)
            mixer = (mixer_keep_ref[place].astype(F32) + mixer_recv_ref[place].astype(F32)).astype(BF16)
            block = mixer.shape[0] // 2
            for other in range(4):
                piece = mixer[:, other * high : (other + 1) * high]
                target[step, flip(other ^ me_n), high:, :] = jnp.concatenate(
                    [piece[0:block, :], piece[block : 2 * block, :]], axis=1
                )
            return carry

        lax.fori_loop(0, 2, one_slot, 0)


def expand_grads(place, normed_own, normed_other, grad_hidden, mixer_keep, mixer_recv):
    rows, width = normed_own.shape
    out = shape((2, 4, width // 4 + width // 16, grad_hidden.shape[1] // 4), BF16)
    return call(
        expand_grads_kernel,
        [out, out],
        place, normed_own, normed_other, grad_hidden, mixer_keep, mixer_recv,
        scratch=[pltpu.VMEM((width, 2 * rows), BF16), pltpu.VMEM((width, 2 * rows), BF16)],
        name="expand_grads",
    )


def triple_grads_kernel(
    place_ref, x0_ref, x1_ref, x2_ref, x3_ref, near_ref, far_ref, normed_ref, grad_triple_ref, sums_in_ref,
    t0_ref, t1_ref, t2_ref, t3_ref, packet_ref, sums_ref,
    weight_ref,
):
    me, corner = place_ref[0], place_ref[7]
    rows, width = normed_ref.shape
    part = grad_triple_ref.shape[2]
    def sum_block(step, sums):
        here = rows_at(step, 64)
        gain_sum, shift_sum = sums
        for slot, x_ref in enumerate((x0_ref, x1_ref, x2_ref, x3_ref)):
            unit, _ = unit_rows(x_ref[here, :].astype(F32))
            grad = (near_ref if slot < 2 else far_ref)[slot % 2, here, :].astype(F32)
            gain_sum += (grad * unit).reshape(8, 8, width).sum(axis=0)
            shift_sum += grad.reshape(8, 8, width).sum(axis=0)
        return gain_sum, shift_sum

    gain_sum, shift_sum = lax.fori_loop(
        0, rows // 256, sum_block, (jnp.zeros((8, width), F32), jnp.zeros((8, width), F32))
    )
    gain_sum, shift_sum = column_sum(gain_sum), column_sum(shift_sum)
    sums_ref[0:16, :] = sums_in_ref[...]
    sums_ref[16:24, :] = jnp.zeros((8, width), F32)
    sums_ref[SUM_FRONT_GAIN : SUM_FRONT_GAIN + 1, :] = gain_sum
    sums_ref[SUM_FRONT_SHIFT : SUM_FRONT_SHIFT + 1, :] = shift_sum
    group = lax.broadcasted_iota(jnp.int32, (1, width), 1) // part
    for row, index in ((0, 0), (1, 2)):
        bias = column_sum(grad_triple_ref[index].astype(F32))
        sums_ref[SUM_TRIPLE + row : SUM_TRIPLE + row + 1, :] = jnp.where(
            group == me, jnp.concatenate([bias] * (width // part), axis=1), 0.0
        )
    for index in range(3):
        weight_ref[index * part : (index + 1) * part, :] = dot(grad_triple_ref[index], normed_ref[...], TN).astype(BF16)
    piece = 3 * part // 4
    for slot, target in enumerate((t0_ref, t1_ref, t2_ref, t3_ref)):
        target[...] = weight_ref[rows_at(corner ^ slot, piece), :]
    local = far_ref.shape[1]
    packet_ref[0:local, :] = far_ref[0]
    packet_ref[local : 2 * local, :] = far_ref[1]
    put_sums(packet_ref, 2 * local, sums_ref[...])


def triple_grads(place, shards, near, far, normed, grad_triple, sums):
    rows, width = normed.shape
    part = grad_triple.shape[2]
    return call(
        triple_grads_kernel,
        [shape((3 * part // 4, width), BF16)] * 4
        + [shape((rows // 2 + 2 * SUMS, width), BF16), shape((SUMS, width), F32)],
        place, *shards, near, far, normed, grad_triple, sums,
        scratch=[pltpu.VMEM((3 * part, width), BF16)],
        vmem=16,
        name="triple_grads",
    )


def pair_kernel(place_ref, near_ref, sent_ref, recv_ref, packet_ref, own_ref):
    local = near_ref.shape[1]
    own_ref[...] = near_ref[0].astype(F32) + recv_ref[0:local, :].astype(F32)
    packet_ref[0:local, :] = (near_ref[1].astype(F32) + recv_ref[local : 2 * local, :].astype(F32)).astype(BF16)
    put_sums(packet_ref, local, get_sums(sent_ref, 2 * local) + get_sums(recv_ref, 2 * local))


def pair_part(place, near, sent, recv):
    _, local, width = near.shape
    return call(
        pair_kernel,
        [shape((local + 2 * SUMS, width), BF16), shape((local, width), F32)],
        place, near, sent, recv,
        name="pair_part",
    )


def home_kernel(place_ref, t0_ref, t1_ref, t2_ref, t3_ref, sent_ref, recv_ref, packet_ref):
    piece = t0_ref.shape[0]
    local = sent_ref.shape[0] - 2 * SUMS
    total = t0_ref[...].astype(F32) + t1_ref[...].astype(F32) + t2_ref[...].astype(F32) + t3_ref[...].astype(F32)
    packet_ref[0:piece, :] = total.astype(BF16)
    put_sums(packet_ref, piece, get_sums(sent_ref, local) + get_sums(recv_ref, local))


def home_part(place, pieces, sent, recv):
    piece, width = pieces[0].shape
    return call(
        home_kernel, [shape((piece + 2 * SUMS, width), BF16)], place, *pieces, sent, recv, name="home_part"
    )[0]


def front_kernel(place_ref, x_ref, own_ref, recv_ref, grad_middle_ref, vectors_ref, out_ref):
    unit, scale = unit_rows(x_ref[...].astype(F32))
    grad = own_ref[...] + recv_ref[0 : own_ref.shape[0], :].astype(F32)
    back = norm_pullback(grad, unit, scale, vector(vectors_ref, FRONT_GAIN))
    out_ref[...] = (grad_middle_ref[...] + back).astype(BF16)


def front_part(place, x, *arrays):
    return call(front_kernel, [shape(x.shape, BF16)], place, x, *arrays, name="front_part")[0]


def spread_kernel(place_ref, sent_ref, recv_ref, packet_ref):
    piece = sent_ref.shape[0] - 2 * SUMS
    packet_ref[0:piece, :] = (sent_ref[0:piece, :].astype(F32) + recv_ref[0:piece, :].astype(F32)).astype(BF16)
    put_sums(packet_ref, piece, get_sums(sent_ref, piece) + get_sums(recv_ref, piece))


def spread_part(place, sent, recv):
    return call(spread_kernel, [shape(sent.shape, BF16)], place, sent, recv, name="spread_part")[0]


def last_kernel(place_ref, s0_ref, s1_ref, s2_ref, s3_ref, a_ref, b_ref, c_ref, packet_ref, total_ref):
    side, corner = place_ref[1], place_ref[7]
    piece = s0_ref.shape[0] - 2 * SUMS
    for slot, ref in enumerate((s0_ref, s1_ref, s2_ref, s3_ref)):
        packet_ref[rows_at(corner ^ slot, piece), :] = ref[0:piece, :]
    put_sums(
        packet_ref,
        4 * piece,
        (get_sums(s0_ref, piece) + get_sums(s1_ref, piece)) + (get_sums(s2_ref, piece) + get_sums(s3_ref, piece)),
    )
    total_ref[...] = a_ref[0].astype(F32) + b_ref[0].astype(F32) + c_ref[...].astype(F32)
    half = (packet_ref.shape[0] - 4 * piece - 2 * SUMS)
    chunk = total_ref.shape[1]
    start = 4 * piece + 2 * SUMS
    packet_ref[start:, 0:chunk] = total_ref[rows_at(2 * (1 - side), half), :].astype(BF16)
    packet_ref[start:, chunk : 2 * chunk] = total_ref[rows_at(2 * (1 - side) + 1, half), :].astype(BF16)


def last_part(place, packets, a, b, c):
    rows, width = packets[0].shape
    piece = rows - 2 * SUMS
    block = width // 8
    return call(
        last_kernel,
        [shape((4 * piece + 2 * SUMS + block // 2, width), BF16), shape(c.shape, F32)],
        place, *packets, a, b, c,
        name="last_part",
    )


def results_kernel(
    place_ref, sent_ref, recv_ref, total_ref, ra_ref, rb_ref, rc_ref, layer_ref, rows_ref,
    triple_ref, expand_ref, mixer_ref, reduce_ref, layer_out_ref, rows_out_ref, triple_bias_ref, table_ref,
    front_gain_ref, front_shift_ref, mixer_bias_ref, back_gain_ref, back_shift_ref, expand_bias_ref, reduce_bias_ref,
    sums_ref,
):
    side, me_n, stay = place_ref[1], place_ref[3], place_ref[5]
    layer_out_ref[...] = layer_ref[...]
    rows_out_ref[...] = rows_ref[...]
    weights, width = triple_ref.shape
    part = mixer_ref.shape[1]

    @pl.when(stay == 1)
    def _():
        triple_ref[...] = sent_ref[0:weights, :].astype(F32)
        sums_ref[...] = get_sums(sent_ref, weights)

    @pl.when(stay == 0)
    def _():
        triple_ref[...] = recv_ref[0:weights, :].astype(F32)
        sums_ref[...] = get_sums(recv_ref, weights)

    block, double = expand_ref.shape
    chunk, half = double // 2, block // 2
    start = weights + 2 * SUMS
    for index in range(2):
        mine = total_ref[rows_at(2 * side + index, half), :]
        other = recv_ref[start:, index * chunk : (index + 1) * chunk].astype(F32)
        first = jnp.full(mine.shape, side, jnp.int32) == 0
        here = slice(index * half, (index + 1) * half)
        expand_ref[here, 0:chunk] = jnp.where(first, mine, other)
        expand_ref[here, chunk:double] = jnp.where(first, other, mine)
        mixer_ref[here, :] = total_ref[2 * block :, index * part : (index + 1) * part]
    reduce_ref[...] = ra_ref[0].astype(F32) + rb_ref[0].astype(F32) + rc_ref[...].astype(F32)
    pair = sums_ref[SUM_TRIPLE : SUM_TRIPLE + 2, :]
    bias = jnp.zeros((2, part), F32)
    for group in range(width // part):
        mine = jnp.full(bias.shape, me_n, jnp.int32) == group
        bias = jnp.where(mine, pair[:, group * part : (group + 1) * part], bias)
    triple_bias_ref[...] = bias
    table_ref[...] = sums_ref[SUM_TABLE : SUM_TABLE + table_ref.shape[0], :]
    for index, ref in (
        (SUM_FRONT_GAIN, front_gain_ref), (SUM_FRONT_SHIFT, front_shift_ref), (SUM_MIXER, mixer_bias_ref),
        (SUM_GAIN, back_gain_ref), (SUM_SHIFT, back_shift_ref), (SUM_COT, reduce_bias_ref),
    ):
        ref[...] = sums_ref[index : index + 1, :].reshape(width)
    for index in range(4):
        expand_bias_ref[index * width : (index + 1) * width] = (
            sums_ref[SUM_EXPAND + index : SUM_EXPAND + index + 1, :].reshape(width)
        )


def results(place, sent, recv, total, ra, rb, rc, layer, rows, passes):
    width = sent.shape[1]
    block = width // 8
    piece = (sent.shape[0] - 2 * SUMS - block // 2) // 4
    row = shape((width,), F32)
    return call(
        results_kernel,
        [
            shape((4 * piece, width), F32), shape((block, width), F32), shape((block, width // 4), F32),
            shape(rc.shape, F32), shape(layer.shape, BF16), shape(rows.shape, BF16),
            shape((2, width // 4), F32), shape((passes, width), F32),
            row, row, row, row, row, shape((4 * width,), F32), row,
        ],
        place, sent, recv, total, ra, rb, rc, layer, rows,
        scratch=[pltpu.VMEM((SUMS, width), F32)],
        name="results",
    )


def after(value, *earlier):
    return lax.optimization_barrier((value, earlier))[0]


def body(
    inputs,
    pass_ids,
    front_gain,
    front_shift,
    triple_weight,
    triple_bias,
    mixer_weight,
    mixer_bias,
    back_gain,
    back_shift,
    expand_weight,
    expand_bias,
    reduce_weight,
    reduce_bias,
    pass_table,
    cotangent,
):
    width = inputs.shape[1]
    part = triple_weight.shape[2]
    wide_size, narrow_size = lax.axis_size("wide"), lax.axis_size("narrow")
    low_bits = wide_size.bit_length() - 4
    side_bit, x_bit, y_bit = 1 << low_bits, 2 << low_bits, 4 << low_bits

    wide, narrow = lax.axis_index("wide"), lax.axis_index("narrow")
    c, h, l = wide & 1, narrow >> 1, narrow & 1
    me = 2 * c + l
    top = wide >> low_bits
    side, quarter = top & 1, top >> 1
    x1, y1 = (wide >> 1) & 1, (wide >> 2) & 1
    stay = (c == h).astype(jnp.int32)
    corner = 2 * y1 + x1
    place = jnp.stack(
        [
            me, side, quarter, narrow,
            jnp.where(c == 0, 2 * x1 + y1, corner),
            stay,
            jnp.where(h == 0, 2 * x1 + y1, corner),
            corner,
        ]
    ).astype(jnp.int32)

    def send(name, value, target):
        pairs = []
        for w in range(wide_size):
            for n in range(narrow_size):
                to = target(w, n)
                if to is not None:
                    pairs.append((w * narrow_size + n, to[0] * narrow_size + to[1]))
        with jax.named_scope(name):
            return lax.ppermute(value, AXES, pairs)

    def stays(w, n):
        return (w & 1) == (n >> 1)

    def moved(w, n):
        return (w, n) if stays(w, n) else (w ^ 1, n ^ 2)

    def home(w, n):
        return None if stays(w, n) else (w, n ^ 2)

    def lend(w, n):
        return (w, n ^ 2) if stays(w, n) else None

    def core(w, n):
        return (w ^ 1, n)

    def pair(w, n):
        return (w, n ^ 1)

    def diagonal(w, n):
        return (w ^ 1, n ^ 1)

    def across(w, n):
        return (w, n ^ 2)

    def sided(w, n):
        return (w ^ side_bit, n)

    def first(w, n):
        return (w ^ (y_bit if w & side_bit else x_bit), n)

    def second(w, n):
        return (w ^ (x_bit if w & side_bit else y_bit), n)

    def step_x(w, n):
        return (w ^ 2, n)

    def step_y(w, n):
        return (w ^ 4, n)

    def step_xy(w, n):
        return (w ^ 6, n)

    def of_stay(target):
        return lambda w, n: target(w, n) if stays(w, n) else None

    def of_moved(target):
        return lambda w, n: None if stays(w, n) else target(w, n)

    def add(*terms):
        return sum(t.astype(F32) for t in terms).astype(BF16)

    together = lax.optimization_barrier

    weight_t = jnp.swapaxes(triple_weight, 1, 2).reshape(3 * part, width)
    piece = 3 * part // 4
    lent = lax.dynamic_slice_in_dim(weight_t, corner * piece, piece)
    place, lent = together((place, lent))
    p0 = send("lend_weight", lent, lend)
    x0 = send("rows_move", after(inputs, lent), moved)
    x1_stay = send("rows_pair", inputs, of_stay(pair))
    vectors, tail = gather_vectors(
        place, triple_bias, pass_ids,
        front_gain, front_shift, mixer_bias, back_gain, back_shift, reduce_bias, expand_bias, pass_table,
    )
    tail = send("tail_move", tail, moved)
    x0, p0, x1_stay, vectors, tail = together((x0, p0, x1_stay, vectors, tail))
    x1_moved = send("rows_pair", x0, of_moved(pair))
    p1, p2, p3 = (send("lent", p0, of_moved(step)) for step in (step_x, step_y, step_xy))
    x1_moved, p1, p2, p3 = together((x1_moved, p1, p2, p3))
    x1_rows = jnp.where(stay == 1, x1_stay, x1_moved)
    x2 = send("rows_core", x0, core)
    x3 = send("pair_core", x1_rows, core)
    cot_own = send("cot_move", after(cotangent, x1_rows), moved)

    shards = (x0, x1_rows, x2, x3)
    m0, m1, m2, m3, mixed_t, normed, triple, weight = attend_forward(
        place, shards, tail, vectors, weight_t, (p0, p1, p2, p3)
    )
    m1, m2, m3, cot_own = together(
        (send("m_pair", m1, pair), send("m_core", m2, core), send("m_diagonal", m3, diagonal), cot_own)
    )
    cot_other = send("cot_core", cot_own, sided)
    normed_two, middle, mixed_rows = mixer_part(place, (m0, m1, m2, m3), x0, mixer_weight, vectors, reduce_weight)
    normed_other, cot_other = together((send("normed_core", normed_two, sided), cot_other))
    second_own, grad_own, feed_send, active, grad_hidden, bias_sums = feed_part(
        place, normed_two, normed_other, cot_own, cot_other, expand_weight, reduce_weight, vectors
    )
    feed_recv = send("feed_core", feed_send, sided)
    reduce_send, reduce_keep = reduce_grads(place, cot_own, cot_other, active)
    grad_own, feed_recv, reduce_send = together((grad_own, feed_recv, reduce_send))
    reduce_first = send("reduce_first", reduce_send, first)
    grad_middle, grad_low, g0, g1, g2, g3 = joint_part(
        place, grad_own, feed_recv, middle, cot_own, mixer_weight, vectors
    )
    g1, g2, g3 = send("g_pair", g1, pair), send("g_core", g2, core), send("g_diagonal", g3, diagonal)
    out_rows, sums, mixer_send, mixer_keep = outer_part(
        place, second_own, grad_own, feed_recv, middle, cot_own, grad_low, mixed_rows, tail, vectors, bias_sums,
        seq_rows=pass_ids.shape[1],
    )
    mixer_recv = send("mixer_core", mixer_send, sided)
    expand_send, expand_keep = expand_grads(
        place, normed_two, normed_other, grad_hidden, mixer_keep, mixer_recv
    )
    g1, g2, g3, expand_send, expand_keep, out_rows, reduce_first = together(
        (g1, g2, g3, expand_send, expand_keep, out_rows, reduce_first)
    )
    reduce_second = send("reduce_second", add(reduce_keep[1], reduce_first[1]), second)
    expand_first = send("expand_first", expand_send, first)
    layer_out = send("out_move", out_rows, moved)
    near, far, grad_triple_rows = attend_backward(
        place, (g0, g1, g2, g3), triple, mixed_t, tail, weight
    )

    def halved(keep, first_recv, second_recv):
        return (
            add(keep[0, 0:2], first_recv[0, 0:2], second_recv[0:2]),
            add(keep[0, 2:4], first_recv[0, 2:4], second_recv[2:4]),
        )

    far, near, grad_triple_rows, reduce_second, layer_out = together(
        (far, near, grad_triple_rows, reduce_second, layer_out)
    )
    reduce_a, reduce_b = halved(reduce_keep, reduce_first, reduce_second)
    reduce_pair = send("reduce_pair", reduce_b, pair)
    t0, t1, t2, t3, core_packet, all_sums = triple_grads(place, shards, near, far, normed, grad_triple_rows, sums)
    core_recv, expand_first, reduce_pair = together((send("far_core", core_packet, core), expand_first, reduce_pair))

    pair_packet, own_rows = pair_part(place, near, core_packet, core_recv)
    pair_recv = send("near_pair", pair_packet, pair)
    t1, t2, t3 = send("triple_x", t1, step_x), send("triple_y", t2, step_y), send("triple_xy", t3, step_xy)
    expand_second = send("expand_second", add(expand_keep[1], expand_first[1]), second)
    reduce_across = send("reduce_across", add(reduce_a[1], reduce_pair[1]), across)
    t1, t2, t3, pair_recv, expand_second, reduce_across = together(
        (t1, t2, t3, pair_recv, expand_second, reduce_across)
    )

    home_packet = home_part(place, (t0, t1, t2, t3), pair_packet, pair_recv)
    home_recv = send("triple_home", home_packet, home)
    grad_rows = front_part(place, x0, own_rows, pair_recv, grad_middle, vectors)
    grad_inputs = send("rows_home", grad_rows, moved)
    expand_a, expand_b = halved(expand_keep, expand_first, expand_second)
    expand_pair = send("expand_pair", expand_b, pair)
    home_recv, expand_pair, grad_rows = together((home_recv, expand_pair, grad_rows))

    spread = spread_part(place, home_packet, home_recv)
    s1, s2, s3 = (send("triple_spread", spread, of_stay(step)) for step in (step_x, step_y, step_xy))
    expand_across = send("expand_across", add(expand_a[1], expand_pair[1]), across)
    s1, s2, s3, expand_across, grad_inputs = together((s1, s2, s3, expand_across, grad_inputs))

    last_packet, total = last_part(place, (spread, s1, s2, s3), expand_a, expand_pair, expand_across)
    last_recv = send("last_core", last_packet, core)
    (
        grad_triple, total_expand, total_mixer, total_reduce, layer_out, grad_inputs, grad_triple_bias, grad_table,
        grad_front_gain, grad_front_shift, grad_mixer_bias, grad_back_gain, grad_back_shift, grad_expand_bias,
        grad_reduce_bias,
    ) = results(
        place, last_packet, last_recv, total, reduce_a, reduce_pair, reduce_across, layer_out, grad_inputs,
        pass_table.shape[0],
    )
    grad_triple = jnp.swapaxes(grad_triple.reshape(3, part, width), 1, 2)
    if low_bits:
        size = 1 << low_bits
        peers = [[size * i + j for j in range(size)] for i in range(wide_size // size)]
        total_expand, total_reduce, total_mixer = (
            lax.psum_scatter(t, "wide", scatter_dimension=d, axis_index_groups=peers, tiled=True)
            for t, d in ((total_expand, 0), (total_reduce, 1), (total_mixer, 0))
        )
        peers = [[i + 8 * j for j in range(wide_size // 8)] for i in range(8)]
        (
            grad_triple, grad_triple_bias, grad_table, grad_front_gain, grad_front_shift, grad_mixer_bias,
            grad_back_gain, grad_back_shift, grad_expand_bias, grad_reduce_bias,
        ) = lax.psum(
            (
                grad_triple, grad_triple_bias, grad_table, grad_front_gain, grad_front_shift, grad_mixer_bias,
                grad_back_gain, grad_back_shift, grad_expand_bias, grad_reduce_bias,
            ),
            "wide", axis_index_groups=peers,
        )
    return (
        layer_out,
        grad_inputs,
        grad_front_gain,
        grad_front_shift,
        grad_triple,
        grad_triple_bias,
        total_mixer,
        grad_mixer_bias,
        grad_back_gain,
        grad_back_shift,
        total_expand,
        grad_expand_bias,
        total_reduce.T,
        grad_reduce_bias,
        grad_table,
    )


def solution(mesh):
    rows = P(AXES, None)
    block = P("wide", "narrow")
    return jax.shard_map(
        body,
        mesh=mesh,
        in_specs=(
            rows, P("wide", None), P(), P(), P(None, None, "narrow"), P(None, "narrow"),
            P(), P(), P(), P(), P(), P(), P(), P(), P(), rows,
        ),
        out_specs=(
            rows, rows, P(), P(), P(None, None, "narrow"), P(None, "narrow"), block,
            P(), P(), P(), block, P(), block, P(), P(),
        ),
        check_vma=False,
    )
```

profile of v0, /device:TPU:3, one launch (start us, length us, event | category | flops | bytes accessed | tf_op | source)
XLA Modules:
  0.0 194.4 jit_solution(2797677644073008722)
XLA Ops:
  1.8 4.8 %collective-permute-start = (bf16[320,768]{1,0:T(8,128)(2,1)}, bf16[320,768]{1,0:T(8,128)(2,1)S(1)}, u32[]{:S(2)}, u32[]{:S(2)}) collective-permute-start(bf16[320,768]{1,0:T(8,128)(2,1)} %param.16), channel_id=1, source_target_pairs={{0,0},{1,1},{2,4},{3,5},{4,2},{5,3},{6,6},{7,7},{8,8},{9,9},{10,12... | collective-permute-start | bytes 1474568 | tf_op jit(solution)/shard_map/rows_move/ppermute | solution.py:869
  18.0 5.8 %collective-permute-done.3.tail_ref = bf16[16,768]{1,0:T(8,128)(2,1)S(1)} collective-permute-done((bf16[16,768]{1,0:T(8,128)(2,1)S(1)}, bf16[16,768]{1,0:T(8,128)(2,1)S(1)}, u32[]{:S(2)}, u32[]{:S(2)}) %collective-permute-start.3) | collective-permute-done | bytes 24608 | tf_op jit(solution)/shard_map/tail_move/ppermute | solution.py:869
  23.8 2.4 %collective-permute-start.4 = (bf16[320,768]{1,0:T(8,128)(2,1)S(1)}, bf16[320,768]{1,0:T(8,128)(2,1)S(1)}, u32[]{:S(2)}, u32[]{:S(2)}) collective-permute-start(bf16[320,768]{1,0:T(8,128)(2,1)S(1)} %collective-permute-done.x0_ref.x_ref), channel_id=1, source_target_pairs={{2,3},{3,2},{4,5},{5,4},{10,11},{11,10},{12,13},{13,12},{18,19},{1... | collective-permute-start | bytes 1474568 | tf_op jit(solution)/shard_map/rows_pair/ppermute | solution.py:869
  26.2 3.1 %collective-permute-start.7 = (bf16[144,768]{1,0:T(8,128)(2,1)S(1)}, bf16[144,768]{1,0:T(8,128)(2,1)S(1)}, u32[]{:S(2)}, u32[]{:S(2)}) collective-permute-start(bf16[144,768]{1,0:T(8,128)(2,1)S(1)} %collective-permute-done.1.p0_ref), channel_id=1, source_target_pairs={{2,26},{3,27},{4,28},{5,29},{10,18},{11,19},{12,20},{13,21},{18,10... | collective-permute-start | bytes 663560 | tf_op jit(solution)/shard_map/lent/ppermute | solution.py:869
  31.5 3.1 %collective-permute-start.5 = (bf16[144,768]{1,0:T(8,128)(2,1)S(1)}, bf16[144,768]{1,0:T(8,128)(2,1)S(1)}, u32[]{:S(2)}, u32[]{:S(2)}) collective-permute-start(bf16[144,768]{1,0:T(8,128)(2,1)S(1)} %collective-permute-done.1.p0_ref), channel_id=1, source_target_pairs={{2,10},{3,11},{4,12},{5,13},{10,2},{11,3},{12,4},{13,5},{18,26},{1... | collective-permute-start | bytes 663560 | tf_op jit(solution)/shard_map/lent/ppermute | solution.py:869
  38.3 7.5 %collective-permute-start.13 = (bf16[320,768]{1,0:T(8,128)(2,1)}, bf16[320,768]{1,0:T(8,128)(2,1)S(1)}, u32[]{:S(2)}, u32[]{:S(2)}) collective-permute-start(bf16[320,768]{1,0:T(8,128)(2,1)} %param.31), channel_id=1, source_target_pairs={{0,0},{1,1},{2,4},{3,5},{4,2},{5,3},{6,6},{7,7},{8,8},{9,9},{10,12... | collective-permute-start | bytes 1474568 | tf_op jit(solution)/shard_map/cot_move/ppermute | solution.py:869
  45.9 13.4 %attend_forward.1 = (bf16[160,384]{1,0:T(8,128)(2,1)S(1)}, bf16[160,384]{1,0:T(8,128)(2,1)S(1)}, bf16[160,384]{1,0:T(8,128)(2,1)S(1)}, bf16[160,384]{1,0:T(8,128...) custom-call(s32[8]{0:T(128)S(1)} %stack.35.place_ref, ...), custom_call_target="tpu_custom_call" | custom-call | tf_op jit(solution)/shard_map/attend_forward/pallas_call | solution.py:42
  61.3 2.5 %collective-permute-done.10.m1_ref = bf16[160,384]{1,0:T(8,128)(2,1)S(1)} collective-permute-done((bf16[160,384]{1,0:T(8,128)(2,1)S(1)}, bf16[160,384]{1,0:T(8,128)(2,1)S(1)}, u32[]{:S(2)}, u32[]{:S(2)}) %collective-permute-start.10) | collective-permute-done | bytes 122912 | tf_op jit(solution)/shard_map/m_pair/ppermute | solution.py:869
  71.3 11.8 %feed_part.1 = (f32[320,768]{1,0:T(8,128)S(1)}, f32[320,768]{1,0:T(8,128)S(1)}, bf16[2,320,768]{2,1,0:T(8,128)(2,1)S(1)}, bf16[640,1536]{1,0:T(8,128)(2,1)S(1)},...) custom-call(s32[8]{0:T(128)S(1)} %stack.35.place_ref, bf16[320,768]{1,0:T(8,128)(2,1)S(1)} %get-tuple-element.147.normed_own_ref, ...), custom_call_target="tpu_custom_call" | custom-call | tf_op jit(solution)/shard_map/feed_part/pallas_call | solution.py:42
  83.3 4.1 %reduce_grads.1 = (bf16[2,4,192,384]{3,2,1,0:T(8,128)(2,1)S(1)}, bf16[2,4,192,384]{3,2,1,0:T(8,128)(2,1)S(1)}) custom-call(s32[8]{0:T(128)S(1)} %stack.35.place_ref, bf16[320,768]{1,0:T(8,128)(2,1)S(1)} %collective-permute-done.13.cot_own_ref.cot_ref, bf16[320,768]{1,0:T(8,128)(2,1)S(1)} %collective-permute-done.15.cot_other_ref, ...), custom_call_target="tpu_custom_call" | custom-call | tf_op jit(solution)/shard_map/reduce_grads/pallas_call | solution.py:42
  90.6 2.2 %outer_part.1 = (bf16[320,768]{1,0:T(8,128)(2,1)S(1)}, f32[16,768]{1,0:T(8,128)S(1)}, bf16[4,96,768]{2,1,0:T(8,128)(2,1)S(1)}, bf16[4,96,768]{2,1,0:T(8,128)(2,1)S(1)}) custom-call(s32[8]{0:T(128)S(1)} %stack.35.place_ref, f32[320,768]{1,0:T(8,128)S(1)} %get-tuple-element.163.second_ref, f32[320,768]{1,0:T(8,128)S(1)} %get-tuple-element.155.grad_own_ref, ...), custom_call_target="tpu_custom_call" | custom-call | tf_op jit(solution)/shard_map/outer_part/pallas_call | solution.py:42
  95.4 4.5 %expand_grads.1 = (bf16[2,4,240,384]{3,2,1,0:T(8,128)(2,1)S(1)}, bf16[2,4,240,384]{3,2,1,0:T(8,128)(2,1)S(1)}) custom-call(s32[8]{0:T(128)S(1)} %stack.35.place_ref, bf16[320,768]{1,0:T(8,128)(2,1)S(1)} %get-tuple-element.147.normed_own_ref, bf16[320,768]{1,0:T(8,128)(2,1)S(1)} %collective-permute-done.14.normed_other_ref, ...), custom_call_target="tpu_custom_call" | custom-call | tf_op jit(solution)/shard_map/expand_grads/pallas_call | solution.py:42
  104.3 3.8 %collective-permute-start.23 = (bf16[320,768]{1,0:T(8,128)(2,1)S(1)}, bf16[320,768]{1,0:T(8,128)(2,1)S(1)}, u32[]{:S(2)}, u32[]{:S(2)}) collective-permute-start(bf16[320,768]{1,0:T(8,128)(2,1)S(1)} %get-tuple-element.184), channel_id=1, source_target_pairs={{0,0},{1,1},{2,4},{3,5},{4,2},{5,3},{6,6},{7,7},{8,8},{9,9},{10,12... | collective-permute-start | bytes 1474568 | tf_op jit(solution)/shard_map/out_move/ppermute | solution.py:869
  108.4 10.7 %attend_backward.1 = (bf16[2,320,768]{2,1,0:T(8,128)(2,1)S(1)}, bf16[2,320,768]{2,1,0:T(8,128)(2,1)S(1)}, bf16[3,1280,192]{2,1,0:T(8,128)(2,1)S(1)}) custom-call(s32[8]{0:T(128)S(1)} %stack.35.place_ref, bf16[160,384]{1,0:T(8,128)(2,1)S(1)} %get-tuple-element.158.g0_ref, bf16[160,384]{1,0:T(8,128)(2,1)S(1)} %collective-permute-done.17.g1_ref, ...), custom_call_target="tpu_custom_call" | custom-call | tf_op jit(solution)/shard_map/attend_backward/pallas_call | solution.py:42
  120.6 4.9 %triple_grads.1 = (bf16[144,768]{1,0:T(8,128)(2,1)S(1)}, bf16[144,768]{1,0:T(8,128)(2,1)S(1)}, bf16[144,768]{1,0:T(8,128)(2,1)S(1)}, bf16[144,768]{1,0:T(8,128)(...) custom-call(s32[8]{0:T(128)S(1)} %stack.35.place_ref, bf16[320,768]{1,0:T(8,128)(2,1)S(1)} %collective-permute-done.x0_ref.x_ref, ...), custom_call_target="tpu_custom_call" | custom-call | tf_op jit(solution)/shard_map/triple_grads/pallas_call | solution.py:42
  125.8 8.0 %collective-permute-done.29.rb_ref = bf16[2,192,384]{2,1,0:T(8,128)(2,1)S(1)} collective-permute-done((bf16[2,192,384]{2,1,0:T(8,128)(2,1)S(1)}, bf16[2,192,384]{2,1,0:T(8,128)(2,1)S(1)}, u32[]{:S(2)}, u32[]{:S(2)}) %collective-permute-start.29) | collective-permute-done | bytes 294944 | tf_op jit(solution)/shard_map/reduce_pair/ppermute | solution.py:869
  138.2 13.6 %collective-permute-done.24.t1_ref = bf16[144,768]{1,0:T(8,128)(2,1)S(1)} collective-permute-done((bf16[144,768]{1,0:T(8,128)(2,1)S(1)}, bf16[144,768]{1,0:T(8,128)(2,1)S(1)}, u32[]{:S(2)}, u32[]{:S(2)}) %collective-permute-start.24) | collective-permute-done | bytes 221216 | tf_op jit(solution)/shard_map/triple_x/ppermute | solution.py:869
  155.0 3.3 %collective-permute-done.32.rc_ref = bf16[192,384]{1,0:T(8,128)(2,1)S(1)} collective-permute-done((bf16[192,384]{1,0:T(8,128)(2,1)S(1)}, bf16[192,384]{1,0:T(8,128)(2,1)S(1)}, u32[]{:S(2)}, u32[]{:S(2)}) %collective-permute-start.32) | collective-permute-done | bytes 147488 | tf_op jit(solution)/shard_map/reduce_across/ppermute | solution.py:869
  159.3 4.5 %collective-permute-start.33 = (bf16[192,768]{1,0:T(8,128)(2,1)S(1)}, bf16[192,768]{1,0:T(8,128)(2,1)S(1)}, u32[]{:S(2)}, u32[]{:S(2)}) collective-permute-start(bf16[192,768]{1,0:T(8,128)(2,1)S(1)} %home_part.1.sent_ref), channel_id=1, source_target_pairs={{2,0},{3,1},{4,6},{5,7},{10,8},{11,9},{12,14},{13,15},{18,16},{19,... | collective-permute-start | bytes 884744 | tf_op jit(solution)/shard_map/triple_home/ppermute | solution.py:869
  173.5 7.4 %collective-permute-start.38 = (bf16[240,384]{1,0:T(8,128)(2,1)S(1)}, bf16[240,384]{1,0:T(8,128)(2,1)S(1)}, u32[]{:S(2)}, u32[]{:S(2)}) collective-permute-start(bf16[240,384]{1,0:T(8,128)(2,1)S(1)} %fusion.6), channel_id=1, source_target_pairs={{0,2},{1,3},{2,0},{3,1},{4,6},{5,7},{6,4},{7,5},{8,10},{9,11},{10,... | collective-permute-start | bytes 552968 | tf_op jit(solution)/shard_map/expand_across/ppermute | solution.py:869
  181.5 3.1 %collective-permute-done.38.c_ref = bf16[240,384]{1,0:T(8,128)(2,1)S(1)} collective-permute-done((bf16[240,384]{1,0:T(8,128)(2,1)S(1)}, bf16[240,384]{1,0:T(8,128)(2,1)S(1)}, u32[]{:S(2)}, u32[]{:S(2)}) %collective-permute-start.38) | collective-permute-done | bytes 184352 | tf_op jit(solution)/shard_map/expand_across/ppermute | solution.py:869
  185.4 3.9 %collective-permute-start.40 = (bf16[672,768]{1,0:T(8,128)(2,1)S(1)}, bf16[672,768]{1,0:T(8,128)(2,1)S(1)}, u32[]{:S(2)}, u32[]{:S(2)}) collective-permute-start(bf16[672,768]{1,0:T(8,128)(2,1)S(1)} %get-tuple-element.215.sent_ref), channel_id=1, source_target_pairs={{0,4},{1,5},{2,6},{3,7},{4,0},{5,1},{6,2},{7,3},{8,12},{9,13},{10,... | collective-permute-start | bytes 3096584 | tf_op jit(solution)/shard_map/last_core/ppermute | solution.py:869
  189.2 2.3 %collective-permute-done.40.recv_ref = bf16[672,768]{1,0:T(8,128)(2,1)S(1)} collective-permute-done((bf16[672,768]{1,0:T(8,128)(2,1)S(1)}, bf16[672,768]{1,0:T(8,128)(2,1)S(1)}, u32[]{:S(2)}, u32[]{:S(2)}) %collective-permute-start.40) | collective-permute-done | bytes 1032224 | tf_op jit(solution)/shard_map/last_core/ppermute | solution.py:869
  191.5 2.7 %results.1 = (f32[576,768]{1,0:T(8,128)}, f32[96,768]{1,0:T(8,128)}, f32[96,192]{1,0:T(8,128)}, f32[192,384]{1,0:T(8,128)}, bf16[320,768]{1,0:T(8,128)(2,1)}, /*...) custom-call(s32[8]{0:T(128)S(1)} %stack.35.place_ref, ...), custom_call_target="tpu_custom_call" | custom-call | tf_op jit(solution)/shard_map/results/pallas_call | solution.py:42
  (113 shorter events, 59.8 us)
Async XLA Ops:
  1.8 22.0 %collective-permute-start = (bf16[320,768]{1,0:T(8,128)(2,1)}, bf16[320,768]{1,0:T(8,128)(2,1)S(1)}, u32[]{:S(2)}, u32[]{:S(2)}) collective-permute-start(bf16[320,768]{1,0:T(8,128)(2,1)} %param.16), channel_id=1, source_target_pairs={{0,0},{1,1},{2,4},{3,5},{4,2},{5,3},{6,6},{7,7},{8,8},{9,9},{10,12... | collective-permute-start | bytes 1474568 | tf_op jit(solution)/shard_map/rows_move/ppermute | solution.py:869
  6.6 17.3 %collective-permute-start.2 = (bf16[320,768]{1,0:T(8,128)(2,1)}, bf16[320,768]{1,0:T(8,128)(2,1)S(1)}, u32[]{:S(2)}, u32[]{:S(2)}) collective-permute-start(bf16[320,768]{1,0:T(8,128)(2,1)} %param.16), channel_id=1, source_target_pairs={{0,1},{1,0},{6,7},{7,6},{8,9},{9,8},{14,15},{15,14},{16,17},{17,16... | collective-permute-start | bytes 1474568 | tf_op jit(solution)/shard_map/rows_pair/ppermute | solution.py:869
  7.3 16.5 %collective-permute-start.1 = (bf16[144,768]{1,0:T(8,128)(2,1)S(1)}, bf16[144,768]{1,0:T(8,128)(2,1)S(1)}, u32[]{:S(2)}, u32[]{:S(2)}) collective-permute-start(bf16[144,768]{1,0:T(8,128)(2,1)S(1)} %constant_dynamic-slice_fusion), channel_id=1, source_target_pairs={{0,2},{1,3},{6,4},{7,5},{8,10},{9,11},{14,12},{15,13},{16,18},{17,... | collective-permute-start | bytes 663560 | tf_op jit(solution)/shard_map/lend_weight/ppermute | solution.py:869
  23.8 14.3 %collective-permute-start.4 = (bf16[320,768]{1,0:T(8,128)(2,1)S(1)}, bf16[320,768]{1,0:T(8,128)(2,1)S(1)}, u32[]{:S(2)}, u32[]{:S(2)}) collective-permute-start(bf16[320,768]{1,0:T(8,128)(2,1)S(1)} %collective-permute-done.x0_ref.x_ref), channel_id=1, source_target_pairs={{2,3},{3,2},{4,5},{5,4},{10,11},{11,10},{12,13},{13,12},{18,19},{1... | collective-permute-start | bytes 1474568 | tf_op jit(solution)/shard_map/rows_pair/ppermute | solution.py:869
  26.2 8.5 %collective-permute-start.7 = (bf16[144,768]{1,0:T(8,128)(2,1)S(1)}, bf16[144,768]{1,0:T(8,128)(2,1)S(1)}, u32[]{:S(2)}, u32[]{:S(2)}) collective-permute-start(bf16[144,768]{1,0:T(8,128)(2,1)S(1)} %collective-permute-done.1.p0_ref), channel_id=1, source_target_pairs={{2,26},{3,27},{4,28},{5,29},{10,18},{11,19},{12,20},{13,21},{18,10... | collective-permute-start | bytes 663560 | tf_op jit(solution)/shard_map/lent/ppermute | solution.py:869
  34.6 11.2 %collective-permute-start.8 = (bf16[320,768]{1,0:T(8,128)(2,1)S(1)}, bf16[320,768]{1,0:T(8,128)(2,1)S(1)}, u32[]{:S(2)}, u32[]{:S(2)}) collective-permute-start(bf16[320,768]{1,0:T(8,128)(2,1)S(1)} %collective-permute-done.x0_ref.x_ref), channel_id=1, source_target_pairs={{0,4},{1,5},{2,6},{3,7},{4,0},{5,1},{6,2},{7,3},{8,12},{9,13},{10,... | collective-permute-start | bytes 1474568 | tf_op jit(solution)/shard_map/rows_core/ppermute | solution.py:869
  38.3 22.9 %collective-permute-start.13 = (bf16[320,768]{1,0:T(8,128)(2,1)}, bf16[320,768]{1,0:T(8,128)(2,1)S(1)}, u32[]{:S(2)}, u32[]{:S(2)}) collective-permute-start(bf16[320,768]{1,0:T(8,128)(2,1)} %param.31), channel_id=1, source_target_pairs={{0,0},{1,1},{2,4},{3,5},{4,2},{5,3},{6,6},{7,7},{8,8},{9,9},{10,12... | collective-permute-start | bytes 1474568 | tf_op jit(solution)/shard_map/cot_move/ppermute | solution.py:869
  87.4 15.4 %collective-permute-start.21 = (bf16[2,4,192,384]{3,2,1,0:T(8,128)(2,1)S(1)}, bf16[2,4,192,384]{3,2,1,0:T(8,128)(2,1)S(1)}, u32[]{:S(2)}, u32[]{:S(2)}) collective-permute-start(bf16[2,4,192,384]{3,2,1,0:T(8,128)(2,1)S(1)} %get-tuple-element.172), channel_id=1, source_target_pairs={{0,8},{1,9},{2,10},{3,11},{4,20},{5,21},{6,22},{7,23},{8,0},{9,1},... | collective-permute-start | bytes 3538952 | tf_op jit(solution)/shard_map/reduce_first/ppermute | solution.py:869
  103.0 17.6 %collective-permute-start.22 = (bf16[4,192,384]{2,1,0:T(8,128)(2,1)S(1)}, bf16[4,192,384]{2,1,0:T(8,128)(2,1)S(1)}, u32[]{:S(2)}, u32[]{:S(2)}) collective-permute-start(bf16[4,192,384]{2,1,0:T(8,128)(2,1)S(1)} %fusion.3), channel_id=1, source_target_pairs={{0,16},{1,17},{2,18},{3,19},{4,12},{5,13},{6,14},{7,15},{8,24},{9,... | collective-permute-start | bytes 1769480 | tf_op jit(solution)/shard_map/reduce_second/ppermute | solution.py:869
  104.3 16.3 %collective-permute-start.23 = (bf16[320,768]{1,0:T(8,128)(2,1)S(1)}, bf16[320,768]{1,0:T(8,128)(2,1)S(1)}, u32[]{:S(2)}, u32[]{:S(2)}) collective-permute-start(bf16[320,768]{1,0:T(8,128)(2,1)S(1)} %get-tuple-element.184), channel_id=1, source_target_pairs={{0,0},{1,1},{2,4},{3,5},{4,2},{5,3},{6,6},{7,7},{8,8},{9,9},{10,12... | collective-permute-start | bytes 1474568 | tf_op jit(solution)/shard_map/out_move/ppermute | solution.py:869
  108.1 25.7 %collective-permute-start.28 = (bf16[2,4,240,384]{3,2,1,0:T(8,128)(2,1)S(1)}, bf16[2,4,240,384]{3,2,1,0:T(8,128)(2,1)S(1)}, u32[]{:S(2)}, u32[]{:S(2)}) collective-permute-start(bf16[2,4,240,384]{3,2,1,0:T(8,128)(2,1)S(1)} %get-tuple-element.195), channel_id=1, source_target_pairs={{0,8},{1,9},{2,10},{3,11},{4,20},{5,21},{6,22},{7,23},{8,0},{9,1},... | collective-permute-start | bytes 4423688 | tf_op jit(solution)/shard_map/expand_first/ppermute | solution.py:869
  125.4 8.4 %collective-permute-start.27 = (bf16[688,768]{1,0:T(8,128)(2,1)S(1)}, bf16[688,768]{1,0:T(8,128)(2,1)S(1)}, u32[]{:S(2)}, u32[]{:S(2)}) collective-permute-start(bf16[688,768]{1,0:T(8,128)(2,1)S(1)} %get-tuple-element.194.sent_ref), channel_id=1, source_target_pairs={{0,4},{1,5},{2,6},{3,7},{4,0},{5,1},{6,2},{7,3},{8,12},{9,13},{10,... | collective-permute-start | bytes 3170312 | tf_op jit(solution)/shard_map/far_core/ppermute | solution.py:869
  134.0 24.2 %collective-permute-start.31 = (bf16[4,240,384]{2,1,0:T(8,128)(2,1)S(1)}, bf16[4,240,384]{2,1,0:T(8,128)(2,1)S(1)}, u32[]{:S(2)}, u32[]{:S(2)}) collective-permute-start(bf16[4,240,384]{2,1,0:T(8,128)(2,1)S(1)} %fusion), channel_id=1, source_target_pairs={{0,16},{1,17},{2,18},{3,19},{4,12},{5,13},{6,14},{7,15},{8,24},{9,... | collective-permute-start | bytes 2211848 | tf_op jit(solution)/shard_map/expand_second/ppermute | solution.py:869
  135.2 23.1 %collective-permute-start.30 = (bf16[368,768]{1,0:T(8,128)(2,1)S(1)}, bf16[368,768]{1,0:T(8,128)(2,1)S(1)}, u32[]{:S(2)}, u32[]{:S(2)}) collective-permute-start(bf16[368,768]{1,0:T(8,128)(2,1)S(1)} %get-tuple-element.198.sent_ref), channel_id=1, source_target_pairs={{0,1},{1,0},{2,3},{3,2},{4,5},{5,4},{6,7},{7,6},{8,9},{9,8},{10,11... | collective-permute-start | bytes 1695752 | tf_op jit(solution)/shard_map/near_pair/ppermute | solution.py:869
  135.6 16.3 %collective-permute-start.24 = (bf16[144,768]{1,0:T(8,128)(2,1)S(1)}, bf16[144,768]{1,0:T(8,128)(2,1)S(1)}, u32[]{:S(2)}, u32[]{:S(2)}) collective-permute-start(bf16[144,768]{1,0:T(8,128)(2,1)S(1)} %get-tuple-element.191), channel_id=1, source_target_pairs={{0,8},{1,9},{2,10},{3,11},{4,12},{5,13},{6,14},{7,15},{8,0},{9,1},... | collective-permute-start | bytes 663560 | tf_op jit(solution)/shard_map/triple_x/ppermute | solution.py:869
  136.7 16.4 %collective-permute-start.25 = (bf16[144,768]{1,0:T(8,128)(2,1)S(1)}, bf16[144,768]{1,0:T(8,128)(2,1)S(1)}, u32[]{:S(2)}, u32[]{:S(2)}) collective-permute-start(bf16[144,768]{1,0:T(8,128)(2,1)S(1)} %get-tuple-element.192), channel_id=1, source_target_pairs={{0,16},{1,17},{2,18},{3,19},{4,20},{5,21},{6,22},{7,23},{8,24},{9,... | collective-permute-start | bytes 663560 | tf_op jit(solution)/shard_map/triple_y/ppermute | solution.py:869
  138.0 17.0 %collective-permute-start.26 = (bf16[144,768]{1,0:T(8,128)(2,1)S(1)}, bf16[144,768]{1,0:T(8,128)(2,1)S(1)}, u32[]{:S(2)}, u32[]{:S(2)}) collective-permute-start(bf16[144,768]{1,0:T(8,128)(2,1)S(1)} %get-tuple-element.193), channel_id=1, source_target_pairs={{0,24},{1,25},{2,26},{3,27},{4,28},{5,29},{6,30},{7,31},{8,16},{9,... | collective-permute-start | bytes 663560 | tf_op jit(solution)/shard_map/triple_xy/ppermute | solution.py:869
  158.5 12.2 %collective-permute-start.34 = (bf16[2,240,384]{2,1,0:T(8,128)(2,1)S(1)}, bf16[2,240,384]{2,1,0:T(8,128)(2,1)S(1)}, u32[]{:S(2)}, u32[]{:S(2)}) collective-permute-start(bf16[2,240,384]{2,1,0:T(8,128)(2,1)S(1)} %get-tuple-element.236), channel_id=1, source_target_pairs={{0,1},{1,0},{2,3},{3,2},{4,5},{5,4},{6,7},{7,6},{8,9},{9,8},{10,11... | collective-permute-start | bytes 1105928 | tf_op jit(solution)/shard_map/expand_pair/ppermute | solution.py:869
  159.3 9.5 %collective-permute-start.33 = (bf16[192,768]{1,0:T(8,128)(2,1)S(1)}, bf16[192,768]{1,0:T(8,128)(2,1)S(1)}, u32[]{:S(2)}, u32[]{:S(2)}) collective-permute-start(bf16[192,768]{1,0:T(8,128)(2,1)S(1)} %home_part.1.sent_ref), channel_id=1, source_target_pairs={{2,0},{3,1},{4,6},{5,7},{10,8},{11,9},{12,14},{13,15},{18,16},{19,... | collective-permute-start | bytes 884744 | tf_op jit(solution)/shard_map/triple_home/ppermute | solution.py:869
  165.0 16.5 %collective-permute-start.39 = (bf16[320,768]{1,0:T(8,128)(2,1)S(1)}, bf16[320,768]{1,0:T(8,128)(2,1)S(1)}, u32[]{:S(2)}, u32[]{:S(2)}) collective-permute-start(bf16[320,768]{1,0:T(8,128)(2,1)S(1)} %front_part.1), channel_id=1, source_target_pairs={{0,0},{1,1},{2,4},{3,5},{4,2},{5,3},{6,6},{7,7},{8,8},{9,9},{10,12... | collective-permute-start | bytes 1474568 | tf_op jit(solution)/shard_map/rows_home/ppermute | solution.py:869
  171.3 13.3 %collective-permute-start.37 = (bf16[192,768]{1,0:T(8,128)(2,1)S(1)}, bf16[192,768]{1,0:T(8,128)(2,1)S(1)}, u32[]{:S(2)}, u32[]{:S(2)}) collective-permute-start(bf16[192,768]{1,0:T(8,128)(2,1)S(1)} %spread_part.1.s0_ref), channel_id=1, source_target_pairs={{0,24},{1,25},{6,30},{7,31},{8,16},{9,17},{14,22},{15,23},{16,8},{... | collective-permute-start | bytes 884744 | tf_op jit(solution)/shard_map/triple_spread/ppermute | solution.py:869
  172.0 12.6 %collective-permute-start.36 = (bf16[192,768]{1,0:T(8,128)(2,1)S(1)}, bf16[192,768]{1,0:T(8,128)(2,1)S(1)}, u32[]{:S(2)}, u32[]{:S(2)}) collective-permute-start(bf16[192,768]{1,0:T(8,128)(2,1)S(1)} %spread_part.1.s0_ref), channel_id=1, source_target_pairs={{0,16},{1,17},{6,22},{7,23},{8,24},{9,25},{14,30},{15,31},{16,0},{... | collective-permute-start | bytes 884744 | tf_op jit(solution)/shard_map/triple_spread/ppermute | solution.py:869
  172.7 11.9 %collective-permute-start.35 = (bf16[192,768]{1,0:T(8,128)(2,1)S(1)}, bf16[192,768]{1,0:T(8,128)(2,1)S(1)}, u32[]{:S(2)}, u32[]{:S(2)}) collective-permute-start(bf16[192,768]{1,0:T(8,128)(2,1)S(1)} %spread_part.1.s0_ref), channel_id=1, source_target_pairs={{0,8},{1,9},{6,14},{7,15},{8,0},{9,1},{14,6},{15,7},{16,24},{17,25... | collective-permute-start | bytes 884744 | tf_op jit(solution)/shard_map/triple_spread/ppermute | solution.py:869
  173.5 11.2 %collective-permute-start.38 = (bf16[240,384]{1,0:T(8,128)(2,1)S(1)}, bf16[240,384]{1,0:T(8,128)(2,1)S(1)}, u32[]{:S(2)}, u32[]{:S(2)}) collective-permute-start(bf16[240,384]{1,0:T(8,128)(2,1)S(1)} %fusion.6), channel_id=1, source_target_pairs={{0,2},{1,3},{2,0},{3,1},{4,6},{5,7},{6,4},{7,5},{8,10},{9,11},{10,... | collective-permute-start | bytes 552968 | tf_op jit(solution)/shard_map/expand_across/ppermute | solution.py:869
  (32 other events, 187.4 us)
where the time goes:
time: 198 us; the launch traced here: 194 us
  starting transfers between devices  64.2 us (32%)
  Pallas kernels  62.4 us (32%)
  waiting for transfers between devices  56.3 us (28%)
  local copies, waits for them, and re-layouts  9.25 us (5%)
    ppermute x41, starting transfers between devices, send(): return lax.ppermute(value, AXES, pairs)  64.2 us
    pallas_call x16, Pallas kernels, call(): pl.pallas_call(kernel, out_shape=tuple(outs), in_specs=[pl.BlockSpec(memo...  62.4 us
    ppermute x41, waiting for transfers between devices, send(): return lax.ppermute(value, AXES, pairs)  56.3 us
    unnamed x30, local copies, waits for them, and re-layouts  8.13 us
  transfers between devices with their start and end apart: 41, of which 18 were waited for; matrix products, arithmetic and copies ran while one was open for 0% of the time, Pallas kernels for 24%

commit v1 on v0

--- a/solution.py
+++ b/solution.py
@@ -993,7 +993,8 @@
     reduce_a, reduce_b = halved(reduce_keep, reduce_first, reduce_second)
     reduce_pair = send("reduce_pair", reduce_b, pair)
     t0, t1, t2, t3, core_packet, all_sums = triple_grads(place, shards, near, far, normed, grad_triple_rows, sums)
-    core_recv, expand_first, reduce_pair = together((send("far_core", core_packet, core), expand_first, reduce_pair))
+    core_packet = after(core_packet, reduce_pair)
+    core_recv, expand_first = together((send("far_core", core_packet, core), expand_first))
 
     pair_packet, own_rows = pair_part(place, near, core_packet, core_recv)
     pair_recv = send("near_pair", pair_packet, pair)

time: 198 us -> 194 us (0.980); the launches traced: 194 us -> 193 us
  transfers between devices with their start and end apart: 41 -> 41, of which waited for: 18 -> 19; matrix products, arithmetic and copies ran while one was open for 0% -> 0% of each run, Pallas kernels for 24% -> 24%
where the time goes in v1:
time: 194 us; the launch traced here: 193 us
  starting transfers between devices  63.7 us (33%)
  Pallas kernels  62.4 us (32%)
  waiting for transfers between devices  55.6 us (29%)
  local copies, waits for them, and re-layouts  9.25 us (5%)
    ppermute x41, starting transfers between devices, send(): return lax.ppermute(value, AXES, pairs)  63.7 us
    pallas_call x16, Pallas kernels, call(): pl.pallas_call(kernel, out_shape=tuple(outs), in_specs=[pl.BlockSpec(memo...  62.4 us
    ppermute x41, waiting for transfers between devices, send(): return lax.ppermute(value, AXES, pairs)  55.6 us
    unnamed x30, local copies, waits for them, and re-layouts  8.13 us
  transfers between devices with their start and end apart: 41, of which 19 were waited for; matrix products, arithmetic and copies ran while one was open for 0% of the time, Pallas kernels for 24%

profile of v1, /device:TPU:3, one launch (start us, length us, event | category | flops | bytes accessed | tf_op | source)
XLA Modules:
  0.0 193.3 jit_solution(12607447679845524600)
XLA Ops:
  1.8 4.8 %collective-permute-start = (bf16[320,768]{1,0:T(8,128)(2,1)}, bf16[320,768]{1,0:T(8,128)(2,1)S(1)}, u32[]{:S(2)}, u32[]{:S(2)}) collective-permute-start(bf16[320,768]{1,0:T(8,128)(2,1)} %param.16), channel_id=1, source_target_pairs={{0,0},{1,1},{2,4},{3,5},{4,2},{5,3},{6,6},{7,7},{8,8},{9,9},{10,12... | collective-permute-start | bytes 1474568 | tf_op jit(solution)/shard_map/rows_move/ppermute | solution.py:869
  18.0 5.8 %collective-permute-done.3.tail_ref = bf16[16,768]{1,0:T(8,128)(2,1)S(1)} collective-permute-done((bf16[16,768]{1,0:T(8,128)(2,1)S(1)}, bf16[16,768]{1,0:T(8,128)(2,1)S(1)}, u32[]{:S(2)}, u32[]{:S(2)}) %collective-permute-start.3) | collective-permute-done | bytes 24608 | tf_op jit(solution)/shard_map/tail_move/ppermute | solution.py:869
  23.8 2.4 %collective-permute-start.4 = (bf16[320,768]{1,0:T(8,128)(2,1)S(1)}, bf16[320,768]{1,0:T(8,128)(2,1)S(1)}, u32[]{:S(2)}, u32[]{:S(2)}) collective-permute-start(bf16[320,768]{1,0:T(8,128)(2,1)S(1)} %collective-permute-done.x0_ref.x_ref), channel_id=1, source_target_pairs={{2,3},{3,2},{4,5},{5,4},{10,11},{11,10},{12,13},{13,12},{18,19},{1... | collective-permute-start | bytes 1474568 | tf_op jit(solution)/shard_map/rows_pair/ppermute | solution.py:869
  26.2 3.1 %collective-permute-start.7 = (bf16[144,768]{1,0:T(8,128)(2,1)S(1)}, bf16[144,768]{1,0:T(8,128)(2,1)S(1)}, u32[]{:S(2)}, u32[]{:S(2)}) collective-permute-start(bf16[144,768]{1,0:T(8,128)(2,1)S(1)} %collective-permute-done.1.p0_ref), channel_id=1, source_target_pairs={{2,26},{3,27},{4,28},{5,29},{10,18},{11,19},{12,20},{13,21},{18,10... | collective-permute-start | bytes 663560 | tf_op jit(solution)/shard_map/lent/ppermute | solution.py:869
  31.5 3.1 %collective-permute-start.5 = (bf16[144,768]{1,0:T(8,128)(2,1)S(1)}, bf16[144,768]{1,0:T(8,128)(2,1)S(1)}, u32[]{:S(2)}, u32[]{:S(2)}) collective-permute-start(bf16[144,768]{1,0:T(8,128)(2,1)S(1)} %collective-permute-done.1.p0_ref), channel_id=1, source_target_pairs={{2,10},{3,11},{4,12},{5,13},{10,2},{11,3},{12,4},{13,5},{18,26},{1... | collective-permute-start | bytes 663560 | tf_op jit(solution)/shard_map/lent/ppermute | solution.py:869
  38.3 7.5 %collective-permute-start.13 = (bf16[320,768]{1,0:T(8,128)(2,1)}, bf16[320,768]{1,0:T(8,128)(2,1)S(1)}, u32[]{:S(2)}, u32[]{:S(2)}) collective-permute-start(bf16[320,768]{1,0:T(8,128)(2,1)} %param.31), channel_id=1, source_target_pairs={{0,0},{1,1},{2,4},{3,5},{4,2},{5,3},{6,6},{7,7},{8,8},{9,9},{10,12... | collective-permute-start | bytes 1474568 | tf_op jit(solution)/shard_map/cot_move/ppermute | solution.py:869
  45.9 13.4 %attend_forward.1 = (bf16[160,384]{1,0:T(8,128)(2,1)S(1)}, bf16[160,384]{1,0:T(8,128)(2,1)S(1)}, bf16[160,384]{1,0:T(8,128)(2,1)S(1)}, bf16[160,384]{1,0:T(8,128...) custom-call(s32[8]{0:T(128)S(1)} %stack.35.place_ref, ...), custom_call_target="tpu_custom_call" | custom-call | tf_op jit(solution)/shard_map/attend_forward/pallas_call | solution.py:42
  61.3 2.5 %collective-permute-done.10.m1_ref = bf16[160,384]{1,0:T(8,128)(2,1)S(1)} collective-permute-done((bf16[160,384]{1,0:T(8,128)(2,1)S(1)}, bf16[160,384]{1,0:T(8,128)(2,1)S(1)}, u32[]{:S(2)}, u32[]{:S(2)}) %collective-permute-start.10) | collective-permute-done | bytes 122912 | tf_op jit(solution)/shard_map/m_pair/ppermute | solution.py:869
  71.3 11.8 %feed_part.1 = (f32[320,768]{1,0:T(8,128)S(1)}, f32[320,768]{1,0:T(8,128)S(1)}, bf16[2,320,768]{2,1,0:T(8,128)(2,1)S(1)}, bf16[640,1536]{1,0:T(8,128)(2,1)S(1)},...) custom-call(s32[8]{0:T(128)S(1)} %stack.35.place_ref, bf16[320,768]{1,0:T(8,128)(2,1)S(1)} %get-tuple-element.147.normed_own_ref, ...), custom_call_target="tpu_custom_call" | custom-call | tf_op jit(solution)/shard_map/feed_part/pallas_call | solution.py:42
  83.3 4.1 %reduce_grads.1 = (bf16[2,4,192,384]{3,2,1,0:T(8,128)(2,1)S(1)}, bf16[2,4,192,384]{3,2,1,0:T(8,128)(2,1)S(1)}) custom-call(s32[8]{0:T(128)S(1)} %stack.35.place_ref, bf16[320,768]{1,0:T(8,128)(2,1)S(1)} %collective-permute-done.13.cot_own_ref.cot_ref, bf16[320,768]{1,0:T(8,128)(2,1)S(1)} %collective-permute-done.15.cot_other_ref, ...), custom_call_target="tpu_custom_call" | custom-call | tf_op jit(solution)/shard_map/reduce_grads/pallas_call | solution.py:42
  95.4 4.5 %expand_grads.1 = (bf16[2,4,240,384]{3,2,1,0:T(8,128)(2,1)S(1)}, bf16[2,4,240,384]{3,2,1,0:T(8,128)(2,1)S(1)}) custom-call(s32[8]{0:T(128)S(1)} %stack.35.place_ref, bf16[320,768]{1,0:T(8,128)(2,1)S(1)} %get-tuple-element.147.normed_own_ref, bf16[320,768]{1,0:T(8,128)(2,1)S(1)} %collective-permute-done.14.normed_other_ref, ...), custom_call_target="tpu_custom_call" | custom-call | tf_op jit(solution)/shard_map/expand_grads/pallas_call | solution.py:42
  104.3 3.8 %collective-permute-start.23 = (bf16[320,768]{1,0:T(8,128)(2,1)S(1)}, bf16[320,768]{1,0:T(8,128)(2,1)S(1)}, u32[]{:S(2)}, u32[]{:S(2)}) collective-permute-start(bf16[320,768]{1,0:T(8,128)(2,1)S(1)} %get-tuple-element.184), channel_id=1, source_target_pairs={{0,0},{1,1},{2,4},{3,5},{4,2},{5,3},{6,6},{7,7},{8,8},{9,9},{10,12... | collective-permute-start | bytes 1474568 | tf_op jit(solution)/shard_map/out_move/ppermute | solution.py:869
  108.4 10.7 %attend_backward.1 = (bf16[2,320,768]{2,1,0:T(8,128)(2,1)S(1)}, bf16[2,320,768]{2,1,0:T(8,128)(2,1)S(1)}, bf16[3,1280,192]{2,1,0:T(8,128)(2,1)S(1)}) custom-call(s32[8]{0:T(128)S(1)} %stack.35.place_ref, bf16[160,384]{1,0:T(8,128)(2,1)S(1)} %get-tuple-element.158.g0_ref, bf16[160,384]{1,0:T(8,128)(2,1)S(1)} %collective-permute-done.17.g1_ref, ...), custom_call_target="tpu_custom_call" | custom-call | tf_op jit(solution)/shard_map/attend_backward/pallas_call | solution.py:42
  120.9 4.9 %triple_grads.1 = (bf16[144,768]{1,0:T(8,128)(2,1)S(1)}, bf16[144,768]{1,0:T(8,128)(2,1)S(1)}, bf16[144,768]{1,0:T(8,128)(2,1)S(1)}, bf16[144,768]{1,0:T(8,128)(...) custom-call(s32[8]{0:T(128)S(1)} %stack.35.place_ref, bf16[320,768]{1,0:T(8,128)(2,1)S(1)} %collective-permute-done.x0_ref.x_ref, ...), custom_call_target="tpu_custom_call" | custom-call | tf_op jit(solution)/shard_map/triple_grads/pallas_call | solution.py:42
  125.8 2.7 %collective-permute-done.27.rb_ref = bf16[2,192,384]{2,1,0:T(8,128)(2,1)S(1)} collective-permute-done((bf16[2,192,384]{2,1,0:T(8,128)(2,1)S(1)}, bf16[2,192,384]{2,1,0:T(8,128)(2,1)S(1)}, u32[]{:S(2)}, u32[]{:S(2)}) %collective-permute-start.27) | collective-permute-done | bytes 294944 | tf_op jit(solution)/shard_map/reduce_pair/ppermute | solution.py:869
  135.9 13.3 %collective-permute-done.24.t1_ref = bf16[144,768]{1,0:T(8,128)(2,1)S(1)} collective-permute-done((bf16[144,768]{1,0:T(8,128)(2,1)S(1)}, bf16[144,768]{1,0:T(8,128)(2,1)S(1)}, u32[]{:S(2)}, u32[]{:S(2)}) %collective-permute-start.24) | collective-permute-done | bytes 221216 | tf_op jit(solution)/shard_map/triple_x/ppermute | solution.py:869
  149.2 2.4 %collective-permute-done.26.t3_ref = bf16[144,768]{1,0:T(8,128)(2,1)S(1)} collective-permute-done((bf16[144,768]{1,0:T(8,128)(2,1)S(1)}, bf16[144,768]{1,0:T(8,128)(2,1)S(1)}, u32[]{:S(2)}, u32[]{:S(2)}) %collective-permute-start.26) | collective-permute-done | bytes 221216 | tf_op jit(solution)/shard_map/triple_xy/ppermute | solution.py:869
  151.6 4.0 %collective-permute-done.32.rc_ref = bf16[192,384]{1,0:T(8,128)(2,1)S(1)} collective-permute-done((bf16[192,384]{1,0:T(8,128)(2,1)S(1)}, bf16[192,384]{1,0:T(8,128)(2,1)S(1)}, u32[]{:S(2)}, u32[]{:S(2)}) %collective-permute-start.32) | collective-permute-done | bytes 147488 | tf_op jit(solution)/shard_map/reduce_across/ppermute | solution.py:869
  156.7 2.8 %collective-permute-start.33 = (bf16[192,768]{1,0:T(8,128)(2,1)S(1)}, bf16[192,768]{1,0:T(8,128)(2,1)S(1)}, u32[]{:S(2)}, u32[]{:S(2)}) collective-permute-start(bf16[192,768]{1,0:T(8,128)(2,1)S(1)} %home_part.1.sent_ref), channel_id=1, source_target_pairs={{2,0},{3,1},{4,6},{5,7},{10,8},{11,9},{12,14},{13,15},{18,16},{19,... | collective-permute-start | bytes 884744 | tf_op jit(solution)/shard_map/triple_home/ppermute | solution.py:869
  162.7 2.6 %collective-permute-done.33.recv_ref = bf16[192,768]{1,0:T(8,128)(2,1)S(1)} collective-permute-done((bf16[192,768]{1,0:T(8,128)(2,1)S(1)}, bf16[192,768]{1,0:T(8,128)(2,1)S(1)}, u32[]{:S(2)}, u32[]{:S(2)}) %collective-permute-start.33) | collective-permute-done | bytes 294944 | tf_op jit(solution)/shard_map/triple_home/ppermute | solution.py:869
  169.6 7.8 %collective-permute-start.38 = (bf16[240,384]{1,0:T(8,128)(2,1)S(1)}, bf16[240,384]{1,0:T(8,128)(2,1)S(1)}, u32[]{:S(2)}, u32[]{:S(2)}) collective-permute-start(bf16[240,384]{1,0:T(8,128)(2,1)S(1)} %fusion.6), channel_id=1, source_target_pairs={{0,2},{1,3},{2,0},{3,1},{4,6},{5,7},{6,4},{7,5},{8,10},{9,11},{10,... | collective-permute-start | bytes 552968 | tf_op jit(solution)/shard_map/expand_across/ppermute | solution.py:869
  177.3 4.2 %collective-permute-done.38.c_ref = bf16[240,384]{1,0:T(8,128)(2,1)S(1)} collective-permute-done((bf16[240,384]{1,0:T(8,128)(2,1)S(1)}, bf16[240,384]{1,0:T(8,128)(2,1)S(1)}, u32[]{:S(2)}, u32[]{:S(2)}) %collective-permute-start.38) | collective-permute-done | bytes 184352 | tf_op jit(solution)/shard_map/expand_across/ppermute | solution.py:869
  182.3 5.7 %collective-permute-start.40 = (bf16[672,768]{1,0:T(8,128)(2,1)S(1)}, bf16[672,768]{1,0:T(8,128)(2,1)S(1)}, u32[]{:S(2)}, u32[]{:S(2)}) collective-permute-start(bf16[672,768]{1,0:T(8,128)(2,1)S(1)} %get-tuple-element.215.sent_ref), channel_id=1, source_target_pairs={{0,4},{1,5},{2,6},{3,7},{4,0},{5,1},{6,2},{7,3},{8,12},{9,13},{10,... | collective-permute-start | bytes 3096584 | tf_op jit(solution)/shard_map/last_core/ppermute | solution.py:869
  190.3 2.7 %results.1 = (f32[576,768]{1,0:T(8,128)}, f32[96,768]{1,0:T(8,128)}, f32[96,192]{1,0:T(8,128)}, f32[192,384]{1,0:T(8,128)}, bf16[320,768]{1,0:T(8,128)(2,1)}, /*...) custom-call(s32[8]{0:T(128)S(1)} %stack.35.place_ref, ...), custom_call_target="tpu_custom_call" | custom-call | tf_op jit(solution)/shard_map/results/pallas_call | solution.py:42
  (113 shorter events, 61.2 us)
Async XLA Ops:
  1.8 22.0 %collective-permute-start = (bf16[320,768]{1,0:T(8,128)(2,1)}, bf16[320,768]{1,0:T(8,128)(2,1)S(1)}, u32[]{:S(2)}, u32[]{:S(2)}) collective-permute-start(bf16[320,768]{1,0:T(8,128)(2,1)} %param.16), channel_id=1, source_target_pairs={{0,0},{1,1},{2,4},{3,5},{4,2},{5,3},{6,6},{7,7},{8,8},{9,9},{10,12... | collective-permute-start | bytes 1474568 | tf_op jit(solution)/shard_map/rows_move/ppermute | solution.py:869
  6.6 17.3 %collective-permute-start.2 = (bf16[320,768]{1,0:T(8,128)(2,1)}, bf16[320,768]{1,0:T(8,128)(2,1)S(1)}, u32[]{:S(2)}, u32[]{:S(2)}) collective-permute-start(bf16[320,768]{1,0:T(8,128)(2,1)} %param.16), channel_id=1, source_target_pairs={{0,1},{1,0},{6,7},{7,6},{8,9},{9,8},{14,15},{15,14},{16,17},{17,16... | collective-permute-start | bytes 1474568 | tf_op jit(solution)/shard_map/rows_pair/ppermute | solution.py:869
  7.3 16.5 %collective-permute-start.1 = (bf16[144,768]{1,0:T(8,128)(2,1)S(1)}, bf16[144,768]{1,0:T(8,128)(2,1)S(1)}, u32[]{:S(2)}, u32[]{:S(2)}) collective-permute-start(bf16[144,768]{1,0:T(8,128)(2,1)S(1)} %constant_dynamic-slice_fusion), channel_id=1, source_target_pairs={{0,2},{1,3},{6,4},{7,5},{8,10},{9,11},{14,12},{15,13},{16,18},{17,... | collective-permute-start | bytes 663560 | tf_op jit(solution)/shard_map/lend_weight/ppermute | solution.py:869
  23.8 14.3 %collective-permute-start.4 = (bf16[320,768]{1,0:T(8,128)(2,1)S(1)}, bf16[320,768]{1,0:T(8,128)(2,1)S(1)}, u32[]{:S(2)}, u32[]{:S(2)}) collective-permute-start(bf16[320,768]{1,0:T(8,128)(2,1)S(1)} %collective-permute-done.x0_ref.x_ref), channel_id=1, source_target_pairs={{2,3},{3,2},{4,5},{5,4},{10,11},{11,10},{12,13},{13,12},{18,19},{1... | collective-permute-start | bytes 1474568 | tf_op jit(solution)/shard_map/rows_pair/ppermute | solution.py:869
  26.2 8.5 %collective-permute-start.7 = (bf16[144,768]{1,0:T(8,128)(2,1)S(1)}, bf16[144,768]{1,0:T(8,128)(2,1)S(1)}, u32[]{:S(2)}, u32[]{:S(2)}) collective-permute-start(bf16[144,768]{1,0:T(8,128)(2,1)S(1)} %collective-permute-done.1.p0_ref), channel_id=1, source_target_pairs={{2,26},{3,27},{4,28},{5,29},{10,18},{11,19},{12,20},{13,21},{18,10... | collective-permute-start | bytes 663560 | tf_op jit(solution)/shard_map/lent/ppermute | solution.py:869
  34.6 11.2 %collective-permute-start.8 = (bf16[320,768]{1,0:T(8,128)(2,1)S(1)}, bf16[320,768]{1,0:T(8,128)(2,1)S(1)}, u32[]{:S(2)}, u32[]{:S(2)}) collective-permute-start(bf16[320,768]{1,0:T(8,128)(2,1)S(1)} %collective-permute-done.x0_ref.x_ref), channel_id=1, source_target_pairs={{0,4},{1,5},{2,6},{3,7},{4,0},{5,1},{6,2},{7,3},{8,12},{9,13},{10,... | collective-permute-start | bytes 1474568 | tf_op jit(solution)/shard_map/rows_core/ppermute | solution.py:869
  38.3 22.9 %collective-permute-start.13 = (bf16[320,768]{1,0:T(8,128)(2,1)}, bf16[320,768]{1,0:T(8,128)(2,1)S(1)}, u32[]{:S(2)}, u32[]{:S(2)}) collective-permute-start(bf16[320,768]{1,0:T(8,128)(2,1)} %param.31), channel_id=1, source_target_pairs={{0,0},{1,1},{2,4},{3,5},{4,2},{5,3},{6,6},{7,7},{8,8},{9,9},{10,12... | collective-permute-start | bytes 1474568 | tf_op jit(solution)/shard_map/cot_move/ppermute | solution.py:869
  87.4 15.4 %collective-permute-start.21 = (bf16[2,4,192,384]{3,2,1,0:T(8,128)(2,1)S(1)}, bf16[2,4,192,384]{3,2,1,0:T(8,128)(2,1)S(1)}, u32[]{:S(2)}, u32[]{:S(2)}) collective-permute-start(bf16[2,4,192,384]{3,2,1,0:T(8,128)(2,1)S(1)} %get-tuple-element.172), channel_id=1, source_target_pairs={{0,8},{1,9},{2,10},{3,11},{4,20},{5,21},{6,22},{7,23},{8,0},{9,1},... | collective-permute-start | bytes 3538952 | tf_op jit(solution)/shard_map/reduce_first/ppermute | solution.py:869
  103.0 17.6 %collective-permute-start.22 = (bf16[4,192,384]{2,1,0:T(8,128)(2,1)S(1)}, bf16[4,192,384]{2,1,0:T(8,128)(2,1)S(1)}, u32[]{:S(2)}, u32[]{:S(2)}) collective-permute-start(bf16[4,192,384]{2,1,0:T(8,128)(2,1)S(1)} %fusion.3), channel_id=1, source_target_pairs={{0,16},{1,17},{2,18},{3,19},{4,12},{5,13},{6,14},{7,15},{8,24},{9,... | collective-permute-start | bytes 1769480 | tf_op jit(solution)/shard_map/reduce_second/ppermute | solution.py:869
  104.3 16.3 %collective-permute-start.23 = (bf16[320,768]{1,0:T(8,128)(2,1)S(1)}, bf16[320,768]{1,0:T(8,128)(2,1)S(1)}, u32[]{:S(2)}, u32[]{:S(2)}) collective-permute-start(bf16[320,768]{1,0:T(8,128)(2,1)S(1)} %get-tuple-element.184), channel_id=1, source_target_pairs={{0,0},{1,1},{2,4},{3,5},{4,2},{5,3},{6,6},{7,7},{8,8},{9,9},{10,12... | collective-permute-start | bytes 1474568 | tf_op jit(solution)/shard_map/out_move/ppermute | solution.py:869
  108.1 21.2 %collective-permute-start.29 = (bf16[2,4,240,384]{3,2,1,0:T(8,128)(2,1)S(1)}, bf16[2,4,240,384]{3,2,1,0:T(8,128)(2,1)S(1)}, u32[]{:S(2)}, u32[]{:S(2)}) collective-permute-start(bf16[2,4,240,384]{3,2,1,0:T(8,128)(2,1)S(1)} %get-tuple-element.197), channel_id=1, source_target_pairs={{0,8},{1,9},{2,10},{3,11},{4,20},{5,21},{6,22},{7,23},{8,0},{9,1},... | collective-permute-start | bytes 4423688 | tf_op jit(solution)/shard_map/expand_first/ppermute | solution.py:869
  131.4 24.3 %collective-permute-start.31 = (bf16[4,240,384]{2,1,0:T(8,128)(2,1)S(1)}, bf16[4,240,384]{2,1,0:T(8,128)(2,1)S(1)}, u32[]{:S(2)}, u32[]{:S(2)}) collective-permute-start(bf16[4,240,384]{2,1,0:T(8,128)(2,1)S(1)} %fusion), channel_id=1, source_target_pairs={{0,16},{1,17},{2,18},{3,19},{4,12},{5,13},{6,14},{7,15},{8,24},{9,... | collective-permute-start | bytes 2211848 | tf_op jit(solution)/shard_map/expand_second/ppermute | solution.py:869
  132.8 22.9 %collective-permute-start.30 = (bf16[368,768]{1,0:T(8,128)(2,1)S(1)}, bf16[368,768]{1,0:T(8,128)(2,1)S(1)}, u32[]{:S(2)}, u32[]{:S(2)}) collective-permute-start(bf16[368,768]{1,0:T(8,128)(2,1)S(1)} %get-tuple-element.199.sent_ref), channel_id=1, source_target_pairs={{0,1},{1,0},{2,3},{3,2},{4,5},{5,4},{6,7},{7,6},{8,9},{9,8},{10,11... | collective-permute-start | bytes 1695752 | tf_op jit(solution)/shard_map/near_pair/ppermute | solution.py:869
  133.2 16.0 %collective-permute-start.24 = (bf16[144,768]{1,0:T(8,128)(2,1)S(1)}, bf16[144,768]{1,0:T(8,128)(2,1)S(1)}, u32[]{:S(2)}, u32[]{:S(2)}) collective-permute-start(bf16[144,768]{1,0:T(8,128)(2,1)S(1)} %get-tuple-element.191), channel_id=1, source_target_pairs={{0,8},{1,9},{2,10},{3,11},{4,12},{5,13},{6,14},{7,15},{8,0},{9,1},... | collective-permute-start | bytes 663560 | tf_op jit(solution)/shard_map/triple_x/ppermute | solution.py:869
  134.1 15.1 %collective-permute-start.25 = (bf16[144,768]{1,0:T(8,128)(2,1)S(1)}, bf16[144,768]{1,0:T(8,128)(2,1)S(1)}, u32[]{:S(2)}, u32[]{:S(2)}) collective-permute-start(bf16[144,768]{1,0:T(8,128)(2,1)S(1)} %get-tuple-element.192), channel_id=1, source_target_pairs={{0,16},{1,17},{2,18},{3,19},{4,20},{5,21},{6,22},{7,23},{8,24},{9,... | collective-permute-start | bytes 663560 | tf_op jit(solution)/shard_map/triple_y/ppermute | solution.py:869
  134.7 16.8 %collective-permute-start.26 = (bf16[144,768]{1,0:T(8,128)(2,1)S(1)}, bf16[144,768]{1,0:T(8,128)(2,1)S(1)}, u32[]{:S(2)}, u32[]{:S(2)}) collective-permute-start(bf16[144,768]{1,0:T(8,128)(2,1)S(1)} %get-tuple-element.193), channel_id=1, source_target_pairs={{0,24},{1,25},{2,26},{3,27},{4,28},{5,29},{6,30},{7,31},{8,16},{9,... | collective-permute-start | bytes 663560 | tf_op jit(solution)/shard_map/triple_xy/ppermute | solution.py:869
  155.9 10.9 %collective-permute-start.34 = (bf16[2,240,384]{2,1,0:T(8,128)(2,1)S(1)}, bf16[2,240,384]{2,1,0:T(8,128)(2,1)S(1)}, u32[]{:S(2)}, u32[]{:S(2)}) collective-permute-start(bf16[2,240,384]{2,1,0:T(8,128)(2,1)S(1)} %get-tuple-element.236), channel_id=1, source_target_pairs={{0,1},{1,0},{2,3},{3,2},{4,5},{5,4},{6,7},{7,6},{8,9},{9,8},{10,11... | collective-permute-start | bytes 1105928 | tf_op jit(solution)/shard_map/expand_pair/ppermute | solution.py:869
  156.7 8.6 %collective-permute-start.33 = (bf16[192,768]{1,0:T(8,128)(2,1)S(1)}, bf16[192,768]{1,0:T(8,128)(2,1)S(1)}, u32[]{:S(2)}, u32[]{:S(2)}) collective-permute-start(bf16[192,768]{1,0:T(8,128)(2,1)S(1)} %home_part.1.sent_ref), channel_id=1, source_target_pairs={{2,0},{3,1},{4,6},{5,7},{10,8},{11,9},{12,14},{13,15},{18,16},{19,... | collective-permute-start | bytes 884744 | tf_op jit(solution)/shard_map/triple_home/ppermute | solution.py:869
  160.8 16.6 %collective-permute-start.39 = (bf16[320,768]{1,0:T(8,128)(2,1)S(1)}, bf16[320,768]{1,0:T(8,128)(2,1)S(1)}, u32[]{:S(2)}, u32[]{:S(2)}) collective-permute-start(bf16[320,768]{1,0:T(8,128)(2,1)S(1)} %front_part.1), channel_id=1, source_target_pairs={{0,0},{1,1},{2,4},{3,5},{4,2},{5,3},{6,6},{7,7},{8,8},{9,9},{10,12... | collective-permute-start | bytes 1474568 | tf_op jit(solution)/shard_map/rows_home/ppermute | solution.py:869
  167.5 14.1 %collective-permute-start.37 = (bf16[192,768]{1,0:T(8,128)(2,1)S(1)}, bf16[192,768]{1,0:T(8,128)(2,1)S(1)}, u32[]{:S(2)}, u32[]{:S(2)}) collective-permute-start(bf16[192,768]{1,0:T(8,128)(2,1)S(1)} %spread_part.1.s0_ref), channel_id=1, source_target_pairs={{0,24},{1,25},{6,30},{7,31},{8,16},{9,17},{14,22},{15,23},{16,8},{... | collective-permute-start | bytes 884744 | tf_op jit(solution)/shard_map/triple_spread/ppermute | solution.py:869
  168.2 13.4 %collective-permute-start.36 = (bf16[192,768]{1,0:T(8,128)(2,1)S(1)}, bf16[192,768]{1,0:T(8,128)(2,1)S(1)}, u32[]{:S(2)}, u32[]{:S(2)}) collective-permute-start(bf16[192,768]{1,0:T(8,128)(2,1)S(1)} %spread_part.1.s0_ref), channel_id=1, source_target_pairs={{0,16},{1,17},{6,22},{7,23},{8,24},{9,25},{14,30},{15,31},{16,0},{... | collective-permute-start | bytes 884744 | tf_op jit(solution)/shard_map/triple_spread/ppermute | solution.py:869
  168.8 12.8 %collective-permute-start.35 = (bf16[192,768]{1,0:T(8,128)(2,1)S(1)}, bf16[192,768]{1,0:T(8,128)(2,1)S(1)}, u32[]{:S(2)}, u32[]{:S(2)}) collective-permute-start(bf16[192,768]{1,0:T(8,128)(2,1)S(1)} %spread_part.1.s0_ref), channel_id=1, source_target_pairs={{0,8},{1,9},{6,14},{7,15},{8,0},{9,1},{14,6},{15,7},{16,24},{17,25... | collective-permute-start | bytes 884744 | tf_op jit(solution)/shard_map/triple_spread/ppermute | solution.py:869
  169.6 12.0 %collective-permute-start.38 = (bf16[240,384]{1,0:T(8,128)(2,1)S(1)}, bf16[240,384]{1,0:T(8,128)(2,1)S(1)}, u32[]{:S(2)}, u32[]{:S(2)}) collective-permute-start(bf16[240,384]{1,0:T(8,128)(2,1)S(1)} %fusion.6), channel_id=1, source_target_pairs={{0,2},{1,3},{2,0},{3,1},{4,6},{5,7},{6,4},{7,5},{8,10},{9,11},{10,... | collective-permute-start | bytes 552968 | tf_op jit(solution)/shard_map/expand_across/ppermute | solution.py:869
  182.3 8.0 %collective-permute-start.40 = (bf16[672,768]{1,0:T(8,128)(2,1)S(1)}, bf16[672,768]{1,0:T(8,128)(2,1)S(1)}, u32[]{:S(2)}, u32[]{:S(2)}) collective-permute-start(bf16[672,768]{1,0:T(8,128)(2,1)S(1)} %get-tuple-element.215.sent_ref), channel_id=1, source_target_pairs={{0,4},{1,5},{2,6},{3,7},{4,0},{5,1},{6,2},{7,3},{8,12},{9,13},{10,... | collective-permute-start | bytes 3096584 | tf_op jit(solution)/shard_map/last_core/ppermute | solution.py:869
  (32 other events, 183.5 us)

commit v2 on v1

--- a/solution.py
+++ b/solution.py
@@ -71,13 +71,13 @@
 
 
 def put_sums(packet_ref, start, sums):
-    high = sums.astype(BF16)
-    packet_ref[start : start + SUMS, :] = high
-    packet_ref[start + SUMS : start + 2 * SUMS, :] = (sums - high.astype(F32)).astype(BF16)
+    high = sums.astype(BF16).astype(F32)
+    packet_ref[start : start + 2 * SUMS, :] = jnp.concatenate([high, sums - high], axis=0).astype(BF16)
 
 
 def get_sums(packet_ref, start):
-    return packet_ref[start : start + SUMS, :].astype(F32) + packet_ref[start + SUMS : start + 2 * SUMS, :].astype(F32)
+    both = packet_ref[start : start + 2 * SUMS, :].astype(F32)
+    return both[0:SUMS, :] + both[SUMS : 2 * SUMS, :]
 
 
 def keep_head(block, head, axis):
@@ -126,9 +126,9 @@
     out_ref[...] = jnp.zeros_like(out_ref)
     for index, ref in enumerate(refs[:-4]):
         out_ref[index : index + 1, :] = ref[...].astype(F32).reshape(1, width)
+    long = long_ref[...].astype(F32).reshape(1, long_ref.shape[0])
     for index in range(long_ref.shape[0] // width):
-        part = long_ref[index * width : (index + 1) * width]
-        out_ref[EXPAND_BIAS + index : EXPAND_BIAS + index + 1, :] = part.astype(F32).reshape(1, width)
+        out_ref[EXPAND_BIAS + index : EXPAND_BIAS + index + 1, :] = long[:, index * width : (index + 1) * width]
     out_ref[TABLE : TABLE + table_ref.shape[0], :] = table_ref[...].astype(F32)
     ids = ids_ref[...].astype(F32)
     bias = bias_ref[...].astype(F32)
@@ -177,7 +177,7 @@
             weight_ref[rows_at(corner ^ slot, piece), :] = value[...]
 
     straight_ref[...] = weight_ref[...].T
-    bias = tail_ref[0:1, 0 : 2 * part].astype(F32)
+    bias = tail_ref[...].astype(F32)[0:1, 0 : 2 * part]
     for slot, x_ref in enumerate((x0_ref, x1_ref, x2_ref, x3_ref)):
         here = rows_at(me ^ slot, local)
         unit, _ = unit_rows(x_ref[...].astype(F32))
@@ -742,14 +742,12 @@
 
 
 def results_kernel(
-    place_ref, sent_ref, recv_ref, total_ref, ra_ref, rb_ref, rc_ref, layer_ref, rows_ref,
-    triple_ref, expand_ref, mixer_ref, reduce_ref, layer_out_ref, rows_out_ref, triple_bias_ref, table_ref,
+    place_ref, sent_ref, recv_ref, total_ref,
+    triple_ref, expand_ref, mixer_ref, triple_bias_ref, table_ref,
     front_gain_ref, front_shift_ref, mixer_bias_ref, back_gain_ref, back_shift_ref, expand_bias_ref, reduce_bias_ref,
     sums_ref,
 ):
     side, me_n, stay = place_ref[1], place_ref[3], place_ref[5]
-    layer_out_ref[...] = layer_ref[...]
-    rows_out_ref[...] = rows_ref[...]
     weights, width = triple_ref.shape
     part = mixer_ref.shape[1]
 
@@ -774,7 +772,6 @@
         expand_ref[here, 0:chunk] = jnp.where(first, mine, other)
         expand_ref[here, chunk:double] = jnp.where(first, other, mine)
         mixer_ref[here, :] = total_ref[2 * block :, index * part : (index + 1) * part]
-    reduce_ref[...] = ra_ref[0].astype(F32) + rb_ref[0].astype(F32) + rc_ref[...].astype(F32)
     pair = sums_ref[SUM_TRIPLE : SUM_TRIPLE + 2, :]
     bias = jnp.zeros((2, part), F32)
     for group in range(width // part):
@@ -793,7 +790,22 @@
         )
 
 
-def results(place, sent, recv, total, ra, rb, rc, layer, rows, passes):
+def early_results_kernel(place_ref, ra_ref, rb_ref, rc_ref, layer_ref, rows_ref, reduce_ref, layer_out_ref, rows_out_ref):
+    reduce_ref[...] = ra_ref[0].astype(F32) + rb_ref[0].astype(F32) + rc_ref[...].astype(F32)
+    layer_out_ref[...] = layer_ref[...]
+    rows_out_ref[...] = rows_ref[...]
+
+
+def early_results(place, ra, rb, rc, layer, rows):
+    return call(
+        early_results_kernel,
+        [shape(rc.shape, F32), shape(layer.shape, BF16), shape(rows.shape, BF16)],
+        place, ra, rb, rc, layer, rows,
+        name="early_results",
+    )
+
+
+def results(place, sent, recv, total, passes):
     width = sent.shape[1]
     block = width // 8
     piece = (sent.shape[0] - 2 * SUMS - block // 2) // 4
@@ -802,11 +814,10 @@
         results_kernel,
         [
             shape((4 * piece, width), F32), shape((block, width), F32), shape((block, width // 4), F32),
-            shape(rc.shape, F32), shape(layer.shape, BF16), shape(rows.shape, BF16),
             shape((2, width // 4), F32), shape((passes, width), F32),
             row, row, row, row, row, shape((4 * width,), F32), row,
         ],
-        place, sent, recv, total, ra, rb, rc, layer, rows,
+        place, sent, recv, total,
         scratch=[pltpu.VMEM((SUMS, width), F32)],
         name="results",
     )
@@ -1020,14 +1031,15 @@
 
     last_packet, total = last_part(place, (spread, s1, s2, s3), expand_a, expand_pair, expand_across)
     last_recv = send("last_core", last_packet, core)
+    total_reduce, layer_out, grad_inputs = early_results(
+        place, reduce_a, reduce_pair, after(reduce_across, last_packet), layer_out, grad_inputs
+    )
+    last_recv, total_reduce, layer_out, grad_inputs = together((last_recv, total_reduce, layer_out, grad_inputs))
     (
-        grad_triple, total_expand, total_mixer, total_reduce, layer_out, grad_inputs, grad_triple_bias, grad_table,
+        grad_triple, total_expand, total_mixer, grad_triple_bias, grad_table,
         grad_front_gain, grad_front_shift, grad_mixer_bias, grad_back_gain, grad_back_shift, grad_expand_bias,
         grad_reduce_bias,
-    ) = results(
-        place, last_packet, last_recv, total, reduce_a, reduce_pair, reduce_across, layer_out, grad_inputs,
-        pass_table.shape[0],
-    )
+    ) = results(place, last_packet, last_recv, total, pass_table.shape[0])
     grad_triple = jnp.swapaxes(grad_triple.reshape(3, part, width), 1, 2)
     if low_bits:
         size = 1 << low_bits

time: 194 us -> 194 us (level)
    pallas_call x16 -> x17, Pallas kernels: 62.4 us -> 63.6 us  [call(): pl.pallas_call(kernel, out_shape=tuple(outs), in_specs=[pl.BlockSpec(memo...]
  transfers between devices with their start and end apart: 41 -> 41, of which waited for: 19 -> 19; matrix products, arithmetic and copies ran while one was open for 0% -> 0% of each run, Pallas kernels for 24% -> 25%
where the time goes in v2:
time: 194 us; the launch traced here: 193 us
  Pallas kernels  63.6 us (33%)
  starting transfers between devices  63.5 us (33%)
  waiting for transfers between devices  54.1 us (28%)
  local copies, waits for them, and re-layouts  9.25 us (5%)
    pallas_call x17, Pallas kernels, call(): pl.pallas_call(kernel, out_shape=tuple(outs), in_specs=[pl.BlockSpec(memo...  63.6 us
    ppermute x41, starting transfers between devices, send(): return lax.ppermute(value, AXES, pairs)  63.5 us
    ppermute x41, waiting for transfers between devices, send(): return lax.ppermute(value, AXES, pairs)  54.1 us
    unnamed x30, local copies, waits for them, and re-layouts  8.13 us
  transfers between devices with their start and end apart: 41, of which 19 were waited for; matrix products, arithmetic and copies ran while one was open for 0% of the time, Pallas kernels for 25%

profile of v2, /device:TPU:3, one launch (start us, length us, event | category | flops | bytes accessed | tf_op | source)
XLA Modules:
  0.0 192.8 jit_solution(11200765792050044738)
XLA Ops:
  1.8 4.8 %collective-permute-start = (bf16[320,768]{1,0:T(8,128)(2,1)}, bf16[320,768]{1,0:T(8,128)(2,1)S(1)}, u32[]{:S(2)}, u32[]{:S(2)}) collective-permute-start(bf16[320,768]{1,0:T(8,128)(2,1)} %param.16), channel_id=1, source_target_pairs={{0,0},{1,1},{2,4},{3,5},{4,2},{5,3},{6,6},{7,7},{8,8},{9,9},{10,12... | collective-permute-start | bytes 1474568 | tf_op jit(solution)/shard_map/rows_move/ppermute | solution.py:880
  18.0 5.8 %collective-permute-done.3.tail_ref = bf16[16,768]{1,0:T(8,128)(2,1)S(1)} collective-permute-done((bf16[16,768]{1,0:T(8,128)(2,1)S(1)}, bf16[16,768]{1,0:T(8,128)(2,1)S(1)}, u32[]{:S(2)}, u32[]{:S(2)}) %collective-permute-start.3) | collective-permute-done | bytes 24608 | tf_op jit(solution)/shard_map/tail_move/ppermute | solution.py:880
  23.8 2.4 %collective-permute-start.4 = (bf16[320,768]{1,0:T(8,128)(2,1)S(1)}, bf16[320,768]{1,0:T(8,128)(2,1)S(1)}, u32[]{:S(2)}, u32[]{:S(2)}) collective-permute-start(bf16[320,768]{1,0:T(8,128)(2,1)S(1)} %collective-permute-done.x0_ref.x_ref), channel_id=1, source_target_pairs={{2,3},{3,2},{4,5},{5,4},{10,11},{11,10},{12,13},{13,12},{18,19},{1... | collective-permute-start | bytes 1474568 | tf_op jit(solution)/shard_map/rows_pair/ppermute | solution.py:880
  26.2 3.1 %collective-permute-start.7 = (bf16[144,768]{1,0:T(8,128)(2,1)S(1)}, bf16[144,768]{1,0:T(8,128)(2,1)S(1)}, u32[]{:S(2)}, u32[]{:S(2)}) collective-permute-start(bf16[144,768]{1,0:T(8,128)(2,1)S(1)} %collective-permute-done.1.p0_ref), channel_id=1, source_target_pairs={{2,26},{3,27},{4,28},{5,29},{10,18},{11,19},{12,20},{13,21},{18,10... | collective-permute-start | bytes 663560 | tf_op jit(solution)/shard_map/lent/ppermute | solution.py:880
  31.5 3.1 %collective-permute-start.5 = (bf16[144,768]{1,0:T(8,128)(2,1)S(1)}, bf16[144,768]{1,0:T(8,128)(2,1)S(1)}, u32[]{:S(2)}, u32[]{:S(2)}) collective-permute-start(bf16[144,768]{1,0:T(8,128)(2,1)S(1)} %collective-permute-done.1.p0_ref), channel_id=1, source_target_pairs={{2,10},{3,11},{4,12},{5,13},{10,2},{11,3},{12,4},{13,5},{18,26},{1... | collective-permute-start | bytes 663560 | tf_op jit(solution)/shard_map/lent/ppermute | solution.py:880
  38.3 7.5 %collective-permute-start.13 = (bf16[320,768]{1,0:T(8,128)(2,1)}, bf16[320,768]{1,0:T(8,128)(2,1)S(1)}, u32[]{:S(2)}, u32[]{:S(2)}) collective-permute-start(bf16[320,768]{1,0:T(8,128)(2,1)} %param.31), channel_id=1, source_target_pairs={{0,0},{1,1},{2,4},{3,5},{4,2},{5,3},{6,6},{7,7},{8,8},{9,9},{10,12... | collective-permute-start | bytes 1474568 | tf_op jit(solution)/shard_map/cot_move/ppermute | solution.py:880
  45.9 13.4 %attend_forward.1 = (bf16[160,384]{1,0:T(8,128)(2,1)S(1)}, bf16[160,384]{1,0:T(8,128)(2,1)S(1)}, bf16[160,384]{1,0:T(8,128)(2,1)S(1)}, bf16[160,384]{1,0:T(8,128...) custom-call(s32[8]{0:T(128)S(1)} %stack.35.place_ref, ...), custom_call_target="tpu_custom_call" | custom-call | tf_op jit(solution)/shard_map/attend_forward/pallas_call | solution.py:42
  61.3 2.5 %collective-permute-done.10.m1_ref = bf16[160,384]{1,0:T(8,128)(2,1)S(1)} collective-permute-done((bf16[160,384]{1,0:T(8,128)(2,1)S(1)}, bf16[160,384]{1,0:T(8,128)(2,1)S(1)}, u32[]{:S(2)}, u32[]{:S(2)}) %collective-permute-start.10) | collective-permute-done | bytes 122912 | tf_op jit(solution)/shard_map/m_pair/ppermute | solution.py:880
  71.3 11.8 %feed_part.1 = (f32[320,768]{1,0:T(8,128)S(1)}, f32[320,768]{1,0:T(8,128)S(1)}, bf16[2,320,768]{2,1,0:T(8,128)(2,1)S(1)}, bf16[640,1536]{1,0:T(8,128)(2,1)S(1)},...) custom-call(s32[8]{0:T(128)S(1)} %stack.35.place_ref, bf16[320,768]{1,0:T(8,128)(2,1)S(1)} %get-tuple-element.152.normed_own_ref, ...), custom_call_target="tpu_custom_call" | custom-call | tf_op jit(solution)/shard_map/feed_part/pallas_call | solution.py:42
  83.3 4.1 %reduce_grads.1 = (bf16[2,4,192,384]{3,2,1,0:T(8,128)(2,1)S(1)}, bf16[2,4,192,384]{3,2,1,0:T(8,128)(2,1)S(1)}) custom-call(s32[8]{0:T(128)S(1)} %stack.35.place_ref, bf16[320,768]{1,0:T(8,128)(2,1)S(1)} %collective-permute-done.13.cot_own_ref.cot_ref, bf16[320,768]{1,0:T(8,128)(2,1)S(1)} %collective-permute-done.15.cot_other_ref, ...), custom_call_target="tpu_custom_call" | custom-call | tf_op jit(solution)/shard_map/reduce_grads/pallas_call | solution.py:42
  95.4 4.5 %expand_grads.1 = (bf16[2,4,240,384]{3,2,1,0:T(8,128)(2,1)S(1)}, bf16[2,4,240,384]{3,2,1,0:T(8,128)(2,1)S(1)}) custom-call(s32[8]{0:T(128)S(1)} %stack.35.place_ref, bf16[320,768]{1,0:T(8,128)(2,1)S(1)} %get-tuple-element.152.normed_own_ref, bf16[320,768]{1,0:T(8,128)(2,1)S(1)} %collective-permute-done.14.normed_other_ref, ...), custom_call_target="tpu_custom_call" | custom-call | tf_op jit(solution)/shard_map/expand_grads/pallas_call | solution.py:42
  104.3 3.8 %collective-permute-start.23 = (bf16[320,768]{1,0:T(8,128)(2,1)S(1)}, bf16[320,768]{1,0:T(8,128)(2,1)S(1)}, u32[]{:S(2)}, u32[]{:S(2)}) collective-permute-start(bf16[320,768]{1,0:T(8,128)(2,1)S(1)} %get-tuple-element.189), channel_id=1, source_target_pairs={{0,0},{1,1},{2,4},{3,5},{4,2},{5,3},{6,6},{7,7},{8,8},{9,9},{10,12... | collective-permute-start | bytes 1474568 | tf_op jit(solution)/shard_map/out_move/ppermute | solution.py:880
  108.4 10.7 %attend_backward.1 = (bf16[2,320,768]{2,1,0:T(8,128)(2,1)S(1)}, bf16[2,320,768]{2,1,0:T(8,128)(2,1)S(1)}, bf16[3,1280,192]{2,1,0:T(8,128)(2,1)S(1)}) custom-call(s32[8]{0:T(128)S(1)} %stack.35.place_ref, bf16[160,384]{1,0:T(8,128)(2,1)S(1)} %get-tuple-element.163.g0_ref, bf16[160,384]{1,0:T(8,128)(2,1)S(1)} %collective-permute-done.17.g1_ref, ...), custom_call_target="tpu_custom_call" | custom-call | tf_op jit(solution)/shard_map/attend_backward/pallas_call | solution.py:42
  120.9 4.9 %triple_grads.1 = (bf16[144,768]{1,0:T(8,128)(2,1)S(1)}, bf16[144,768]{1,0:T(8,128)(2,1)S(1)}, bf16[144,768]{1,0:T(8,128)(2,1)S(1)}, bf16[144,768]{1,0:T(8,128)(...) custom-call(s32[8]{0:T(128)S(1)} %stack.35.place_ref, bf16[320,768]{1,0:T(8,128)(2,1)S(1)} %collective-permute-done.x0_ref.x_ref, ...), custom_call_target="tpu_custom_call" | custom-call | tf_op jit(solution)/shard_map/triple_grads/pallas_call | solution.py:42
  125.8 2.7 %collective-permute-done.27.rb_ref = bf16[2,192,384]{2,1,0:T(8,128)(2,1)S(1)} collective-permute-done((bf16[2,192,384]{2,1,0:T(8,128)(2,1)S(1)}, bf16[2,192,384]{2,1,0:T(8,128)(2,1)S(1)}, u32[]{:S(2)}, u32[]{:S(2)}) %collective-permute-start.27) | collective-permute-done | bytes 294944 | tf_op jit(solution)/shard_map/reduce_pair/ppermute | solution.py:880
  135.9 13.3 %collective-permute-done.24.t1_ref = bf16[144,768]{1,0:T(8,128)(2,1)S(1)} collective-permute-done((bf16[144,768]{1,0:T(8,128)(2,1)S(1)}, bf16[144,768]{1,0:T(8,128)(2,1)S(1)}, u32[]{:S(2)}, u32[]{:S(2)}) %collective-permute-start.24) | collective-permute-done | bytes 221216 | tf_op jit(solution)/shard_map/triple_x/ppermute | solution.py:880
  149.2 2.4 %collective-permute-done.26.t3_ref = bf16[144,768]{1,0:T(8,128)(2,1)S(1)} collective-permute-done((bf16[144,768]{1,0:T(8,128)(2,1)S(1)}, bf16[144,768]{1,0:T(8,128)(2,1)S(1)}, u32[]{:S(2)}, u32[]{:S(2)}) %collective-permute-start.26) | collective-permute-done | bytes 221216 | tf_op jit(solution)/shard_map/triple_xy/ppermute | solution.py:880
  151.6 4.0 %collective-permute-done.32.rc_ref = bf16[192,384]{1,0:T(8,128)(2,1)S(1)} collective-permute-done((bf16[192,384]{1,0:T(8,128)(2,1)S(1)}, bf16[192,384]{1,0:T(8,128)(2,1)S(1)}, u32[]{:S(2)}, u32[]{:S(2)}) %collective-permute-start.32) | collective-permute-done | bytes 147488 | tf_op jit(solution)/shard_map/reduce_across/ppermute | solution.py:880
  156.7 2.8 %collective-permute-start.33 = (bf16[192,768]{1,0:T(8,128)(2,1)S(1)}, bf16[192,768]{1,0:T(8,128)(2,1)S(1)}, u32[]{:S(2)}, u32[]{:S(2)}) collective-permute-start(bf16[192,768]{1,0:T(8,128)(2,1)S(1)} %home_part.1.sent_ref), channel_id=1, source_target_pairs={{2,0},{3,1},{4,6},{5,7},{10,8},{11,9},{12,14},{13,15},{18,16},{19,... | collective-permute-start | bytes 884744 | tf_op jit(solution)/shard_map/triple_home/ppermute | solution.py:880
  162.7 2.6 %collective-permute-done.33.recv_ref = bf16[192,768]{1,0:T(8,128)(2,1)S(1)} collective-permute-done((bf16[192,768]{1,0:T(8,128)(2,1)S(1)}, bf16[192,768]{1,0:T(8,128)(2,1)S(1)}, u32[]{:S(2)}, u32[]{:S(2)}) %collective-permute-start.33) | collective-permute-done | bytes 294944 | tf_op jit(solution)/shard_map/triple_home/ppermute | solution.py:880
  169.6 7.8 %collective-permute-start.38 = (bf16[240,384]{1,0:T(8,128)(2,1)S(1)}, bf16[240,384]{1,0:T(8,128)(2,1)S(1)}, u32[]{:S(2)}, u32[]{:S(2)}) collective-permute-start(bf16[240,384]{1,0:T(8,128)(2,1)S(1)} %fusion.6), channel_id=1, source_target_pairs={{0,2},{1,3},{2,0},{3,1},{4,6},{5,7},{6,4},{7,5},{8,10},{9,11},{10,... | collective-permute-start | bytes 552968 | tf_op jit(solution)/shard_map/expand_across/ppermute | solution.py:880
  177.3 4.4 %collective-permute-done.38.c_ref = bf16[240,384]{1,0:T(8,128)(2,1)S(1)} collective-permute-done((bf16[240,384]{1,0:T(8,128)(2,1)S(1)}, bf16[240,384]{1,0:T(8,128)(2,1)S(1)}, u32[]{:S(2)}, u32[]{:S(2)}) %collective-permute-start.38) | collective-permute-done | bytes 184352 | tf_op jit(solution)/shard_map/expand_across/ppermute | solution.py:880
  182.5 5.6 %collective-permute-start.40 = (bf16[672,768]{1,0:T(8,128)(2,1)S(1)}, bf16[672,768]{1,0:T(8,128)(2,1)S(1)}, u32[]{:S(2)}, u32[]{:S(2)}) collective-permute-start(bf16[672,768]{1,0:T(8,128)(2,1)S(1)} %get-tuple-element.220.sent_ref), channel_id=1, source_target_pairs={{0,4},{1,5},{2,6},{3,7},{4,0},{5,1},{6,2},{7,3},{8,12},{9,13},{10,... | collective-permute-start | bytes 3096584 | tf_op jit(solution)/shard_map/last_core/ppermute | solution.py:880
  190.3 2.3 %results.1 = (f32[576,768]{1,0:T(8,128)}, f32[96,768]{1,0:T(8,128)}, f32[96,192]{1,0:T(8,128)}, f32[2,192]{1,0:T(2,128)}, f32[5,768]{1,0:T(8,128)}, /*index=5*/f...) custom-call(s32[8]{0:T(128)S(1)} %stack.35.place_ref, ...), custom_call_target="tpu_custom_call" | custom-call | tf_op jit(solution)/shard_map/results/pallas_call | solution.py:42
  (114 shorter events, 61.2 us)
Async XLA Ops:
  1.8 22.0 %collective-permute-start = (bf16[320,768]{1,0:T(8,128)(2,1)}, bf16[320,768]{1,0:T(8,128)(2,1)S(1)}, u32[]{:S(2)}, u32[]{:S(2)}) collective-permute-start(bf16[320,768]{1,0:T(8,128)(2,1)} %param.16), channel_id=1, source_target_pairs={{0,0},{1,1},{2,4},{3,5},{4,2},{5,3},{6,6},{7,7},{8,8},{9,9},{10,12... | collective-permute-start | bytes 1474568 | tf_op jit(solution)/shard_map/rows_move/ppermute | solution.py:880
  6.6 17.3 %collective-permute-start.2 = (bf16[320,768]{1,0:T(8,128)(2,1)}, bf16[320,768]{1,0:T(8,128)(2,1)S(1)}, u32[]{:S(2)}, u32[]{:S(2)}) collective-permute-start(bf16[320,768]{1,0:T(8,128)(2,1)} %param.16), channel_id=1, source_target_pairs={{0,1},{1,0},{6,7},{7,6},{8,9},{9,8},{14,15},{15,14},{16,17},{17,16... | collective-permute-start | bytes 1474568 | tf_op jit(solution)/shard_map/rows_pair/ppermute | solution.py:880
  7.3 16.5 %collective-permute-start.1 = (bf16[144,768]{1,0:T(8,128)(2,1)S(1)}, bf16[144,768]{1,0:T(8,128)(2,1)S(1)}, u32[]{:S(2)}, u32[]{:S(2)}) collective-permute-start(bf16[144,768]{1,0:T(8,128)(2,1)S(1)} %constant_dynamic-slice_fusion), channel_id=1, source_target_pairs={{0,2},{1,3},{6,4},{7,5},{8,10},{9,11},{14,12},{15,13},{16,18},{17,... | collective-permute-start | bytes 663560 | tf_op jit(solution)/shard_map/lend_weight/ppermute | solution.py:880
  23.8 14.3 %collective-permute-start.4 = (bf16[320,768]{1,0:T(8,128)(2,1)S(1)}, bf16[320,768]{1,0:T(8,128)(2,1)S(1)}, u32[]{:S(2)}, u32[]{:S(2)}) collective-permute-start(bf16[320,768]{1,0:T(8,128)(2,1)S(1)} %collective-permute-done.x0_ref.x_ref), channel_id=1, source_target_pairs={{2,3},{3,2},{4,5},{5,4},{10,11},{11,10},{12,13},{13,12},{18,19},{1... | collective-permute-start | bytes 1474568 | tf_op jit(solution)/shard_map/rows_pair/ppermute | solution.py:880
  26.2 8.5 %collective-permute-start.7 = (bf16[144,768]{1,0:T(8,128)(2,1)S(1)}, bf16[144,768]{1,0:T(8,128)(2,1)S(1)}, u32[]{:S(2)}, u32[]{:S(2)}) collective-permute-start(bf16[144,768]{1,0:T(8,128)(2,1)S(1)} %collective-permute-done.1.p0_ref), channel_id=1, source_target_pairs={{2,26},{3,27},{4,28},{5,29},{10,18},{11,19},{12,20},{13,21},{18,10... | collective-permute-start | bytes 663560 | tf_op jit(solution)/shard_map/lent/ppermute | solution.py:880
  34.6 11.2 %collective-permute-start.8 = (bf16[320,768]{1,0:T(8,128)(2,1)S(1)}, bf16[320,768]{1,0:T(8,128)(2,1)S(1)}, u32[]{:S(2)}, u32[]{:S(2)}) collective-permute-start(bf16[320,768]{1,0:T(8,128)(2,1)S(1)} %collective-permute-done.x0_ref.x_ref), channel_id=1, source_target_pairs={{0,4},{1,5},{2,6},{3,7},{4,0},{5,1},{6,2},{7,3},{8,12},{9,13},{10,... | collective-permute-start | bytes 1474568 | tf_op jit(solution)/shard_map/rows_core/ppermute | solution.py:880
  38.3 22.9 %collective-permute-start.13 = (bf16[320,768]{1,0:T(8,128)(2,1)}, bf16[320,768]{1,0:T(8,128)(2,1)S(1)}, u32[]{:S(2)}, u32[]{:S(2)}) collective-permute-start(bf16[320,768]{1,0:T(8,128)(2,1)} %param.31), channel_id=1, source_target_pairs={{0,0},{1,1},{2,4},{3,5},{4,2},{5,3},{6,6},{7,7},{8,8},{9,9},{10,12... | collective-permute-start | bytes 1474568 | tf_op jit(solution)/shard_map/cot_move/ppermute | solution.py:880
  87.4 15.4 %collective-permute-start.21 = (bf16[2,4,192,384]{3,2,1,0:T(8,128)(2,1)S(1)}, bf16[2,4,192,384]{3,2,1,0:T(8,128)(2,1)S(1)}, u32[]{:S(2)}, u32[]{:S(2)}) collective-permute-start(bf16[2,4,192,384]{3,2,1,0:T(8,128)(2,1)S(1)} %get-tuple-element.177), channel_id=1, source_target_pairs={{0,8},{1,9},{2,10},{3,11},{4,20},{5,21},{6,22},{7,23},{8,0},{9,1},... | collective-permute-start | bytes 3538952 | tf_op jit(solution)/shard_map/reduce_first/ppermute | solution.py:880
  103.0 17.6 %collective-permute-start.22 = (bf16[4,192,384]{2,1,0:T(8,128)(2,1)S(1)}, bf16[4,192,384]{2,1,0:T(8,128)(2,1)S(1)}, u32[]{:S(2)}, u32[]{:S(2)}) collective-permute-start(bf16[4,192,384]{2,1,0:T(8,128)(2,1)S(1)} %fusion.3), channel_id=1, source_target_pairs={{0,16},{1,17},{2,18},{3,19},{4,12},{5,13},{6,14},{7,15},{8,24},{9,... | collective-permute-start | bytes 1769480 | tf_op jit(solution)/shard_map/reduce_second/ppermute | solution.py:880
  104.3 16.3 %collective-permute-start.23 = (bf16[320,768]{1,0:T(8,128)(2,1)S(1)}, bf16[320,768]{1,0:T(8,128)(2,1)S(1)}, u32[]{:S(2)}, u32[]{:S(2)}) collective-permute-start(bf16[320,768]{1,0:T(8,128)(2,1)S(1)} %get-tuple-element.189), channel_id=1, source_target_pairs={{0,0},{1,1},{2,4},{3,5},{4,2},{5,3},{6,6},{7,7},{8,8},{9,9},{10,12... | collective-permute-start | bytes 1474568 | tf_op jit(solution)/shard_map/out_move/ppermute | solution.py:880
  108.1 21.2 %collective-permute-start.29 = (bf16[2,4,240,384]{3,2,1,0:T(8,128)(2,1)S(1)}, bf16[2,4,240,384]{3,2,1,0:T(8,128)(2,1)S(1)}, u32[]{:S(2)}, u32[]{:S(2)}) collective-permute-start(bf16[2,4,240,384]{3,2,1,0:T(8,128)(2,1)S(1)} %get-tuple-element.202), channel_id=1, source_target_pairs={{0,8},{1,9},{2,10},{3,11},{4,20},{5,21},{6,22},{7,23},{8,0},{9,1},... | collective-permute-start | bytes 4423688 | tf_op jit(solution)/shard_map/expand_first/ppermute | solution.py:880
  131.4 24.3 %collective-permute-start.31 = (bf16[4,240,384]{2,1,0:T(8,128)(2,1)S(1)}, bf16[4,240,384]{2,1,0:T(8,128)(2,1)S(1)}, u32[]{:S(2)}, u32[]{:S(2)}) collective-permute-start(bf16[4,240,384]{2,1,0:T(8,128)(2,1)S(1)} %fusion), channel_id=1, source_target_pairs={{0,16},{1,17},{2,18},{3,19},{4,12},{5,13},{6,14},{7,15},{8,24},{9,... | collective-permute-start | bytes 2211848 | tf_op jit(solution)/shard_map/expand_second/ppermute | solution.py:880
  132.8 22.9 %collective-permute-start.30 = (bf16[368,768]{1,0:T(8,128)(2,1)S(1)}, bf16[368,768]{1,0:T(8,128)(2,1)S(1)}, u32[]{:S(2)}, u32[]{:S(2)}) collective-permute-start(bf16[368,768]{1,0:T(8,128)(2,1)S(1)} %get-tuple-element.204.sent_ref), channel_id=1, source_target_pairs={{0,1},{1,0},{2,3},{3,2},{4,5},{5,4},{6,7},{7,6},{8,9},{9,8},{10,11... | collective-permute-start | bytes 1695752 | tf_op jit(solution)/shard_map/near_pair/ppermute | solution.py:880
  133.2 16.0 %collective-permute-start.24 = (bf16[144,768]{1,0:T(8,128)(2,1)S(1)}, bf16[144,768]{1,0:T(8,128)(2,1)S(1)}, u32[]{:S(2)}, u32[]{:S(2)}) collective-permute-start(bf16[144,768]{1,0:T(8,128)(2,1)S(1)} %get-tuple-element.196), channel_id=1, source_target_pairs={{0,8},{1,9},{2,10},{3,11},{4,12},{5,13},{6,14},{7,15},{8,0},{9,1},... | collective-permute-start | bytes 663560 | tf_op jit(solution)/shard_map/triple_x/ppermute | solution.py:880
  134.1 15.1 %collective-permute-start.25 = (bf16[144,768]{1,0:T(8,128)(2,1)S(1)}, bf16[144,768]{1,0:T(8,128)(2,1)S(1)}, u32[]{:S(2)}, u32[]{:S(2)}) collective-permute-start(bf16[144,768]{1,0:T(8,128)(2,1)S(1)} %get-tuple-element.197), channel_id=1, source_target_pairs={{0,16},{1,17},{2,18},{3,19},{4,20},{5,21},{6,22},{7,23},{8,24},{9,... | collective-permute-start | bytes 663560 | tf_op jit(solution)/shard_map/triple_y/ppermute | solution.py:880
  134.7 16.8 %collective-permute-start.26 = (bf16[144,768]{1,0:T(8,128)(2,1)S(1)}, bf16[144,768]{1,0:T(8,128)(2,1)S(1)}, u32[]{:S(2)}, u32[]{:S(2)}) collective-permute-start(bf16[144,768]{1,0:T(8,128)(2,1)S(1)} %get-tuple-element.198), channel_id=1, source_target_pairs={{0,24},{1,25},{2,26},{3,27},{4,28},{5,29},{6,30},{7,31},{8,16},{9,... | collective-permute-start | bytes 663560 | tf_op jit(solution)/shard_map/triple_xy/ppermute | solution.py:880
  155.9 10.9 %collective-permute-start.34 = (bf16[2,240,384]{2,1,0:T(8,128)(2,1)S(1)}, bf16[2,240,384]{2,1,0:T(8,128)(2,1)S(1)}, u32[]{:S(2)}, u32[]{:S(2)}) collective-permute-start(bf16[2,240,384]{2,1,0:T(8,128)(2,1)S(1)} %get-tuple-element.246), channel_id=1, source_target_pairs={{0,1},{1,0},{2,3},{3,2},{4,5},{5,4},{6,7},{7,6},{8,9},{9,8},{10,11... | collective-permute-start | bytes 1105928 | tf_op jit(solution)/shard_map/expand_pair/ppermute | solution.py:880
  156.7 8.6 %collective-permute-start.33 = (bf16[192,768]{1,0:T(8,128)(2,1)S(1)}, bf16[192,768]{1,0:T(8,128)(2,1)S(1)}, u32[]{:S(2)}, u32[]{:S(2)}) collective-permute-start(bf16[192,768]{1,0:T(8,128)(2,1)S(1)} %home_part.1.sent_ref), channel_id=1, source_target_pairs={{2,0},{3,1},{4,6},{5,7},{10,8},{11,9},{12,14},{13,15},{18,16},{19,... | collective-permute-start | bytes 884744 | tf_op jit(solution)/shard_map/triple_home/ppermute | solution.py:880
  160.8 16.6 %collective-permute-start.39 = (bf16[320,768]{1,0:T(8,128)(2,1)S(1)}, bf16[320,768]{1,0:T(8,128)(2,1)S(1)}, u32[]{:S(2)}, u32[]{:S(2)}) collective-permute-start(bf16[320,768]{1,0:T(8,128)(2,1)S(1)} %front_part.1), channel_id=1, source_target_pairs={{0,0},{1,1},{2,4},{3,5},{4,2},{5,3},{6,6},{7,7},{8,8},{9,9},{10,12... | collective-permute-start | bytes 1474568 | tf_op jit(solution)/shard_map/rows_home/ppermute | solution.py:880
  167.5 14.3 %collective-permute-start.37 = (bf16[192,768]{1,0:T(8,128)(2,1)S(1)}, bf16[192,768]{1,0:T(8,128)(2,1)S(1)}, u32[]{:S(2)}, u32[]{:S(2)}) collective-permute-start(bf16[192,768]{1,0:T(8,128)(2,1)S(1)} %spread_part.1.s0_ref), channel_id=1, source_target_pairs={{0,24},{1,25},{6,30},{7,31},{8,16},{9,17},{14,22},{15,23},{16,8},{... | collective-permute-start | bytes 884744 | tf_op jit(solution)/shard_map/triple_spread/ppermute | solution.py:880
  168.2 13.6 %collective-permute-start.36 = (bf16[192,768]{1,0:T(8,128)(2,1)S(1)}, bf16[192,768]{1,0:T(8,128)(2,1)S(1)}, u32[]{:S(2)}, u32[]{:S(2)}) collective-permute-start(bf16[192,768]{1,0:T(8,128)(2,1)S(1)} %spread_part.1.s0_ref), channel_id=1, source_target_pairs={{0,16},{1,17},{6,22},{7,23},{8,24},{9,25},{14,30},{15,31},{16,0},{... | collective-permute-start | bytes 884744 | tf_op jit(solution)/shard_map/triple_spread/ppermute | solution.py:880
  168.8 12.9 %collective-permute-start.35 = (bf16[192,768]{1,0:T(8,128)(2,1)S(1)}, bf16[192,768]{1,0:T(8,128)(2,1)S(1)}, u32[]{:S(2)}, u32[]{:S(2)}) collective-permute-start(bf16[192,768]{1,0:T(8,128)(2,1)S(1)} %spread_part.1.s0_ref), channel_id=1, source_target_pairs={{0,8},{1,9},{6,14},{7,15},{8,0},{9,1},{14,6},{15,7},{16,24},{17,25... | collective-permute-start | bytes 884744 | tf_op jit(solution)/shard_map/triple_spread/ppermute | solution.py:880
  169.6 12.1 %collective-permute-start.38 = (bf16[240,384]{1,0:T(8,128)(2,1)S(1)}, bf16[240,384]{1,0:T(8,128)(2,1)S(1)}, u32[]{:S(2)}, u32[]{:S(2)}) collective-permute-start(bf16[240,384]{1,0:T(8,128)(2,1)S(1)} %fusion.6), channel_id=1, source_target_pairs={{0,2},{1,3},{2,0},{3,1},{4,6},{5,7},{6,4},{7,5},{8,10},{9,11},{10,... | collective-permute-start | bytes 552968 | tf_op jit(solution)/shard_map/expand_across/ppermute | solution.py:880
  182.5 7.9 %collective-permute-start.40 = (bf16[672,768]{1,0:T(8,128)(2,1)S(1)}, bf16[672,768]{1,0:T(8,128)(2,1)S(1)}, u32[]{:S(2)}, u32[]{:S(2)}) collective-permute-start(bf16[672,768]{1,0:T(8,128)(2,1)S(1)} %get-tuple-element.220.sent_ref), channel_id=1, source_target_pairs={{0,4},{1,5},{2,6},{3,7},{4,0},{5,1},{6,2},{7,3},{8,12},{9,13},{10,... | collective-permute-start | bytes 3096584 | tf_op jit(solution)/shard_map/last_core/ppermute | solution.py:880
  (32 other events, 183.6 us)

commit v3 on v2

--- a/solution.py
+++ b/solution.py
@@ -937,7 +937,7 @@
     lent = lax.dynamic_slice_in_dim(weight_t, corner * piece, piece)
     place, lent = together((place, lent))
     p0 = send("lend_weight", lent, lend)
-    x0 = send("rows_move", after(inputs, lent), moved)
+    x0 = send("rows_move", inputs, moved)
     x1_stay = send("rows_pair", inputs, of_stay(pair))
     vectors, tail = gather_vectors(
         place, triple_bias, pass_ids,

time: 194 us -> 193 us (level)
  transfers between devices with their start and end apart: 41 -> 41, of which waited for: 19 -> 19; matrix products, arithmetic and copies ran while one was open for 0% -> 1% of each run, Pallas kernels for 25% -> 25%
where the time goes in v3:
time: 193 us
  starting transfers between devices  63.8 us (33%)
  Pallas kernels  63.6 us (33%)
  waiting for transfers between devices  53.6 us (28%)
  local copies, waits for them, and re-layouts  9.17 us (5%)
    ppermute x41, starting transfers between devices, send(): return lax.ppermute(value, AXES, pairs)  63.8 us
    pallas_call x17, Pallas kernels, call(): pl.pallas_call(kernel, out_shape=tuple(outs), in_specs=[pl.BlockSpec(memo...  63.6 us
    ppermute x41, waiting for transfers between devices, send(): return lax.ppermute(value, AXES, pairs)  53.6 us
    unnamed x30, local copies, waits for them, and re-layouts  8.13 us
  transfers between devices with their start and end apart: 41, of which 19 were waited for; matrix products, arithmetic and copies ran while one was open for 1% of the time, Pallas kernels for 25%

profile of v3, /device:TPU:3, one launch (start us, length us, event | category | flops | bytes accessed | tf_op | source)
XLA Modules:
  0.0 192.5 jit_solution(6633267814133612308)
XLA Ops:
  1.5 4.8 %collective-permute-start = (bf16[320,768]{1,0:T(8,128)(2,1)}, bf16[320,768]{1,0:T(8,128)(2,1)S(1)}, u32[]{:S(2)}, u32[]{:S(2)}) collective-permute-start(bf16[320,768]{1,0:T(8,128)(2,1)} %param.16), channel_id=1, source_target_pairs={{0,0},{1,1},{2,4},{3,5},{4,2},{5,3},{6,6},{7,7},{8,8},{9,9},{10,12... | collective-permute-start | bytes 1474568 | tf_op jit(solution)/shard_map/rows_move/ppermute | solution.py:880
  18.0 5.5 %collective-permute-done.3.tail_ref = bf16[16,768]{1,0:T(8,128)(2,1)S(1)} collective-permute-done((bf16[16,768]{1,0:T(8,128)(2,1)S(1)}, bf16[16,768]{1,0:T(8,128)(2,1)S(1)}, u32[]{:S(2)}, u32[]{:S(2)}) %collective-permute-start.3) | collective-permute-done | bytes 24608 | tf_op jit(solution)/shard_map/tail_move/ppermute | solution.py:880
  23.6 2.4 %collective-permute-start.4 = (bf16[320,768]{1,0:T(8,128)(2,1)S(1)}, bf16[320,768]{1,0:T(8,128)(2,1)S(1)}, u32[]{:S(2)}, u32[]{:S(2)}) collective-permute-start(bf16[320,768]{1,0:T(8,128)(2,1)S(1)} %collective-permute-done.x0_ref.x_ref), channel_id=1, source_target_pairs={{2,3},{3,2},{4,5},{5,4},{10,11},{11,10},{12,13},{13,12},{18,19},{1... | collective-permute-start | bytes 1474568 | tf_op jit(solution)/shard_map/rows_pair/ppermute | solution.py:880
  25.9 3.1 %collective-permute-start.7 = (bf16[144,768]{1,0:T(8,128)(2,1)S(1)}, bf16[144,768]{1,0:T(8,128)(2,1)S(1)}, u32[]{:S(2)}, u32[]{:S(2)}) collective-permute-start(bf16[144,768]{1,0:T(8,128)(2,1)S(1)} %collective-permute-done.1.p0_ref), channel_id=1, source_target_pairs={{2,26},{3,27},{4,28},{5,29},{10,18},{11,19},{12,20},{13,21},{18,10... | collective-permute-start | bytes 663560 | tf_op jit(solution)/shard_map/lent/ppermute | solution.py:880
  31.2 3.1 %collective-permute-start.5 = (bf16[144,768]{1,0:T(8,128)(2,1)S(1)}, bf16[144,768]{1,0:T(8,128)(2,1)S(1)}, u32[]{:S(2)}, u32[]{:S(2)}) collective-permute-start(bf16[144,768]{1,0:T(8,128)(2,1)S(1)} %collective-permute-done.1.p0_ref), channel_id=1, source_target_pairs={{2,10},{3,11},{4,12},{5,13},{10,2},{11,3},{12,4},{13,5},{18,26},{1... | collective-permute-start | bytes 663560 | tf_op jit(solution)/shard_map/lent/ppermute | solution.py:880
  38.0 7.5 %collective-permute-start.13 = (bf16[320,768]{1,0:T(8,128)(2,1)}, bf16[320,768]{1,0:T(8,128)(2,1)S(1)}, u32[]{:S(2)}, u32[]{:S(2)}) collective-permute-start(bf16[320,768]{1,0:T(8,128)(2,1)} %param.31), channel_id=1, source_target_pairs={{0,0},{1,1},{2,4},{3,5},{4,2},{5,3},{6,6},{7,7},{8,8},{9,9},{10,12... | collective-permute-start | bytes 1474568 | tf_op jit(solution)/shard_map/cot_move/ppermute | solution.py:880
  45.6 13.4 %attend_forward.1 = (bf16[160,384]{1,0:T(8,128)(2,1)S(1)}, bf16[160,384]{1,0:T(8,128)(2,1)S(1)}, bf16[160,384]{1,0:T(8,128)(2,1)S(1)}, bf16[160,384]{1,0:T(8,128...) custom-call(s32[8]{0:T(128)S(1)} %stack.35.place_ref, ...), custom_call_target="tpu_custom_call" | custom-call | tf_op jit(solution)/shard_map/attend_forward/pallas_call | solution.py:42
  61.0 2.5 %collective-permute-done.10.m1_ref = bf16[160,384]{1,0:T(8,128)(2,1)S(1)} collective-permute-done((bf16[160,384]{1,0:T(8,128)(2,1)S(1)}, bf16[160,384]{1,0:T(8,128)(2,1)S(1)}, u32[]{:S(2)}, u32[]{:S(2)}) %collective-permute-start.10) | collective-permute-done | bytes 122912 | tf_op jit(solution)/shard_map/m_pair/ppermute | solution.py:880
  71.0 11.8 %feed_part.1 = (f32[320,768]{1,0:T(8,128)S(1)}, f32[320,768]{1,0:T(8,128)S(1)}, bf16[2,320,768]{2,1,0:T(8,128)(2,1)S(1)}, bf16[640,1536]{1,0:T(8,128)(2,1)S(1)},...) custom-call(s32[8]{0:T(128)S(1)} %stack.35.place_ref, bf16[320,768]{1,0:T(8,128)(2,1)S(1)} %get-tuple-element.150.normed_own_ref, ...), custom_call_target="tpu_custom_call" | custom-call | tf_op jit(solution)/shard_map/feed_part/pallas_call | solution.py:42
  83.1 4.1 %reduce_grads.1 = (bf16[2,4,192,384]{3,2,1,0:T(8,128)(2,1)S(1)}, bf16[2,4,192,384]{3,2,1,0:T(8,128)(2,1)S(1)}) custom-call(s32[8]{0:T(128)S(1)} %stack.35.place_ref, bf16[320,768]{1,0:T(8,128)(2,1)S(1)} %collective-permute-done.13.cot_own_ref.cot_ref, bf16[320,768]{1,0:T(8,128)(2,1)S(1)} %collective-permute-done.15.cot_other_ref, ...), custom_call_target="tpu_custom_call" | custom-call | tf_op jit(solution)/shard_map/reduce_grads/pallas_call | solution.py:42
  95.1 4.5 %expand_grads.1 = (bf16[2,4,240,384]{3,2,1,0:T(8,128)(2,1)S(1)}, bf16[2,4,240,384]{3,2,1,0:T(8,128)(2,1)S(1)}) custom-call(s32[8]{0:T(128)S(1)} %stack.35.place_ref, bf16[320,768]{1,0:T(8,128)(2,1)S(1)} %get-tuple-element.150.normed_own_ref, bf16[320,768]{1,0:T(8,128)(2,1)S(1)} %collective-permute-done.14.normed_other_ref, ...), custom_call_target="tpu_custom_call" | custom-call | tf_op jit(solution)/shard_map/expand_grads/pallas_call | solution.py:42
  104.0 3.8 %collective-permute-start.23 = (bf16[320,768]{1,0:T(8,128)(2,1)S(1)}, bf16[320,768]{1,0:T(8,128)(2,1)S(1)}, u32[]{:S(2)}, u32[]{:S(2)}) collective-permute-start(bf16[320,768]{1,0:T(8,128)(2,1)S(1)} %get-tuple-element.187), channel_id=1, source_target_pairs={{0,0},{1,1},{2,4},{3,5},{4,2},{5,3},{6,6},{7,7},{8,8},{9,9},{10,12... | collective-permute-start | bytes 1474568 | tf_op jit(solution)/shard_map/out_move/ppermute | solution.py:880
  108.1 10.7 %attend_backward.1 = (bf16[2,320,768]{2,1,0:T(8,128)(2,1)S(1)}, bf16[2,320,768]{2,1,0:T(8,128)(2,1)S(1)}, bf16[3,1280,192]{2,1,0:T(8,128)(2,1)S(1)}) custom-call(s32[8]{0:T(128)S(1)} %stack.35.place_ref, bf16[160,384]{1,0:T(8,128)(2,1)S(1)} %get-tuple-element.161.g0_ref, bf16[160,384]{1,0:T(8,128)(2,1)S(1)} %collective-permute-done.17.g1_ref, ...), custom_call_target="tpu_custom_call" | custom-call | tf_op jit(solution)/shard_map/attend_backward/pallas_call | solution.py:42
  120.6 4.9 %triple_grads.1 = (bf16[144,768]{1,0:T(8,128)(2,1)S(1)}, bf16[144,768]{1,0:T(8,128)(2,1)S(1)}, bf16[144,768]{1,0:T(8,128)(2,1)S(1)}, bf16[144,768]{1,0:T(8,128)(...) custom-call(s32[8]{0:T(128)S(1)} %stack.35.place_ref, bf16[320,768]{1,0:T(8,128)(2,1)S(1)} %collective-permute-done.x0_ref.x_ref, ...), custom_call_target="tpu_custom_call" | custom-call | tf_op jit(solution)/shard_map/triple_grads/pallas_call | solution.py:42
  125.5 2.7 %collective-permute-done.27.rb_ref = bf16[2,192,384]{2,1,0:T(8,128)(2,1)S(1)} collective-permute-done((bf16[2,192,384]{2,1,0:T(8,128)(2,1)S(1)}, bf16[2,192,384]{2,1,0:T(8,128)(2,1)S(1)}, u32[]{:S(2)}, u32[]{:S(2)}) %collective-permute-start.27) | collective-permute-done | bytes 294944 | tf_op jit(solution)/shard_map/reduce_pair/ppermute | solution.py:880
  135.6 13.3 %collective-permute-done.24.t1_ref = bf16[144,768]{1,0:T(8,128)(2,1)S(1)} collective-permute-done((bf16[144,768]{1,0:T(8,128)(2,1)S(1)}, bf16[144,768]{1,0:T(8,128)(2,1)S(1)}, u32[]{:S(2)}, u32[]{:S(2)}) %collective-permute-start.24) | collective-permute-done | bytes 221216 | tf_op jit(solution)/shard_map/triple_x/ppermute | solution.py:880
  148.8 2.4 %collective-permute-done.26.t3_ref = bf16[144,768]{1,0:T(8,128)(2,1)S(1)} collective-permute-done((bf16[144,768]{1,0:T(8,128)(2,1)S(1)}, bf16[144,768]{1,0:T(8,128)(2,1)S(1)}, u32[]{:S(2)}, u32[]{:S(2)}) %collective-permute-start.26) | collective-permute-done | bytes 221216 | tf_op jit(solution)/shard_map/triple_xy/ppermute | solution.py:880
  151.3 4.0 %collective-permute-done.32.rc_ref = bf16[192,384]{1,0:T(8,128)(2,1)S(1)} collective-permute-done((bf16[192,384]{1,0:T(8,128)(2,1)S(1)}, bf16[192,384]{1,0:T(8,128)(2,1)S(1)}, u32[]{:S(2)}, u32[]{:S(2)}) %collective-permute-start.32) | collective-permute-done | bytes 147488 | tf_op jit(solution)/shard_map/reduce_across/ppermute | solution.py:880
  156.4 2.8 %collective-permute-start.33 = (bf16[192,768]{1,0:T(8,128)(2,1)S(1)}, bf16[192,768]{1,0:T(8,128)(2,1)S(1)}, u32[]{:S(2)}, u32[]{:S(2)}) collective-permute-start(bf16[192,768]{1,0:T(8,128)(2,1)S(1)} %home_part.1.sent_ref), channel_id=1, source_target_pairs={{2,0},{3,1},{4,6},{5,7},{10,8},{11,9},{12,14},{13,15},{18,16},{19,... | collective-permute-start | bytes 884744 | tf_op jit(solution)/shard_map/triple_home/ppermute | solution.py:880
  162.4 2.6 %collective-permute-done.33.recv_ref = bf16[192,768]{1,0:T(8,128)(2,1)S(1)} collective-permute-done((bf16[192,768]{1,0:T(8,128)(2,1)S(1)}, bf16[192,768]{1,0:T(8,128)(2,1)S(1)}, u32[]{:S(2)}, u32[]{:S(2)}) %collective-permute-start.33) | collective-permute-done | bytes 294944 | tf_op jit(solution)/shard_map/triple_home/ppermute | solution.py:880
  169.3 7.8 %collective-permute-start.38 = (bf16[240,384]{1,0:T(8,128)(2,1)S(1)}, bf16[240,384]{1,0:T(8,128)(2,1)S(1)}, u32[]{:S(2)}, u32[]{:S(2)}) collective-permute-start(bf16[240,384]{1,0:T(8,128)(2,1)S(1)} %fusion.6), channel_id=1, source_target_pairs={{0,2},{1,3},{2,0},{3,1},{4,6},{5,7},{6,4},{7,5},{8,10},{9,11},{10,... | collective-permute-start | bytes 552968 | tf_op jit(solution)/shard_map/expand_across/ppermute | solution.py:880
  177.0 4.2 %collective-permute-done.38.c_ref = bf16[240,384]{1,0:T(8,128)(2,1)S(1)} collective-permute-done((bf16[240,384]{1,0:T(8,128)(2,1)S(1)}, bf16[240,384]{1,0:T(8,128)(2,1)S(1)}, u32[]{:S(2)}, u32[]{:S(2)}) %collective-permute-start.38) | collective-permute-done | bytes 184352 | tf_op jit(solution)/shard_map/expand_across/ppermute | solution.py:880
  182.0 5.8 %collective-permute-start.40 = (bf16[672,768]{1,0:T(8,128)(2,1)S(1)}, bf16[672,768]{1,0:T(8,128)(2,1)S(1)}, u32[]{:S(2)}, u32[]{:S(2)}) collective-permute-start(bf16[672,768]{1,0:T(8,128)(2,1)S(1)} %get-tuple-element.218.sent_ref), channel_id=1, source_target_pairs={{0,4},{1,5},{2,6},{3,7},{4,0},{5,1},{6,2},{7,3},{8,12},{9,13},{10,... | collective-permute-start | bytes 3096584 | tf_op jit(solution)/shard_map/last_core/ppermute | solution.py:880
  190.1 2.3 %results.1 = (f32[576,768]{1,0:T(8,128)}, f32[96,768]{1,0:T(8,128)}, f32[96,192]{1,0:T(8,128)}, f32[2,192]{1,0:T(2,128)}, f32[5,768]{1,0:T(8,128)}, /*index=5*/f...) custom-call(s32[8]{0:T(128)S(1)} %stack.35.place_ref, ...), custom_call_target="tpu_custom_call" | custom-call | tf_op jit(solution)/shard_map/results/pallas_call | solution.py:42
  (114 shorter events, 61.2 us)
Async XLA Ops:
  0.7 22.9 %collective-permute-start.2 = (bf16[320,768]{1,0:T(8,128)(2,1)}, bf16[320,768]{1,0:T(8,128)(2,1)S(1)}, u32[]{:S(2)}, u32[]{:S(2)}) collective-permute-start(bf16[320,768]{1,0:T(8,128)(2,1)} %param.16), channel_id=1, source_target_pairs={{0,1},{1,0},{6,7},{7,6},{8,9},{9,8},{14,15},{15,14},{16,17},{17,16... | collective-permute-start | bytes 1474568 | tf_op jit(solution)/shard_map/rows_pair/ppermute | solution.py:880
  1.5 22.1 %collective-permute-start = (bf16[320,768]{1,0:T(8,128)(2,1)}, bf16[320,768]{1,0:T(8,128)(2,1)S(1)}, u32[]{:S(2)}, u32[]{:S(2)}) collective-permute-start(bf16[320,768]{1,0:T(8,128)(2,1)} %param.16), channel_id=1, source_target_pairs={{0,0},{1,1},{2,4},{3,5},{4,2},{5,3},{6,6},{7,7},{8,8},{9,9},{10,12... | collective-permute-start | bytes 1474568 | tf_op jit(solution)/shard_map/rows_move/ppermute | solution.py:880
  7.3 16.2 %collective-permute-start.1 = (bf16[144,768]{1,0:T(8,128)(2,1)S(1)}, bf16[144,768]{1,0:T(8,128)(2,1)S(1)}, u32[]{:S(2)}, u32[]{:S(2)}) collective-permute-start(bf16[144,768]{1,0:T(8,128)(2,1)S(1)} %constant_dynamic-slice_fusion), channel_id=1, source_target_pairs={{0,2},{1,3},{6,4},{7,5},{8,10},{9,11},{14,12},{15,13},{16,18},{17,... | collective-permute-start | bytes 663560 | tf_op jit(solution)/shard_map/lend_weight/ppermute | solution.py:880
  23.6 14.3 %collective-permute-start.4 = (bf16[320,768]{1,0:T(8,128)(2,1)S(1)}, bf16[320,768]{1,0:T(8,128)(2,1)S(1)}, u32[]{:S(2)}, u32[]{:S(2)}) collective-permute-start(bf16[320,768]{1,0:T(8,128)(2,1)S(1)} %collective-permute-done.x0_ref.x_ref), channel_id=1, source_target_pairs={{2,3},{3,2},{4,5},{5,4},{10,11},{11,10},{12,13},{13,12},{18,19},{1... | collective-permute-start | bytes 1474568 | tf_op jit(solution)/shard_map/rows_pair/ppermute | solution.py:880
  25.9 8.5 %collective-permute-start.7 = (bf16[144,768]{1,0:T(8,128)(2,1)S(1)}, bf16[144,768]{1,0:T(8,128)(2,1)S(1)}, u32[]{:S(2)}, u32[]{:S(2)}) collective-permute-start(bf16[144,768]{1,0:T(8,128)(2,1)S(1)} %collective-permute-done.1.p0_ref), channel_id=1, source_target_pairs={{2,26},{3,27},{4,28},{5,29},{10,18},{11,19},{12,20},{13,21},{18,10... | collective-permute-start | bytes 663560 | tf_op jit(solution)/shard_map/lent/ppermute | solution.py:880
  34.3 11.2 %collective-permute-start.8 = (bf16[320,768]{1,0:T(8,128)(2,1)S(1)}, bf16[320,768]{1,0:T(8,128)(2,1)S(1)}, u32[]{:S(2)}, u32[]{:S(2)}) collective-permute-start(bf16[320,768]{1,0:T(8,128)(2,1)S(1)} %collective-permute-done.x0_ref.x_ref), channel_id=1, source_target_pairs={{0,4},{1,5},{2,6},{3,7},{4,0},{5,1},{6,2},{7,3},{8,12},{9,13},{10,... | collective-permute-start | bytes 1474568 | tf_op jit(solution)/shard_map/rows_core/ppermute | solution.py:880
  38.0 22.9 %collective-permute-start.13 = (bf16[320,768]{1,0:T(8,128)(2,1)}, bf16[320,768]{1,0:T(8,128)(2,1)S(1)}, u32[]{:S(2)}, u32[]{:S(2)}) collective-permute-start(bf16[320,768]{1,0:T(8,128)(2,1)} %param.31), channel_id=1, source_target_pairs={{0,0},{1,1},{2,4},{3,5},{4,2},{5,3},{6,6},{7,7},{8,8},{9,9},{10,12... | collective-permute-start | bytes 1474568 | tf_op jit(solution)/shard_map/cot_move/ppermute | solution.py:880
  87.2 15.4 %collective-permute-start.21 = (bf16[2,4,192,384]{3,2,1,0:T(8,128)(2,1)S(1)}, bf16[2,4,192,384]{3,2,1,0:T(8,128)(2,1)S(1)}, u32[]{:S(2)}, u32[]{:S(2)}) collective-permute-start(bf16[2,4,192,384]{3,2,1,0:T(8,128)(2,1)S(1)} %get-tuple-element.175), channel_id=1, source_target_pairs={{0,8},{1,9},{2,10},{3,11},{4,20},{5,21},{6,22},{7,23},{8,0},{9,1},... | collective-permute-start | bytes 3538952 | tf_op jit(solution)/shard_map/reduce_first/ppermute | solution.py:880
  102.7 17.6 %collective-permute-start.22 = (bf16[4,192,384]{2,1,0:T(8,128)(2,1)S(1)}, bf16[4,192,384]{2,1,0:T(8,128)(2,1)S(1)}, u32[]{:S(2)}, u32[]{:S(2)}) collective-permute-start(bf16[4,192,384]{2,1,0:T(8,128)(2,1)S(1)} %fusion.3), channel_id=1, source_target_pairs={{0,16},{1,17},{2,18},{3,19},{4,12},{5,13},{6,14},{7,15},{8,24},{9,... | collective-permute-start | bytes 1769480 | tf_op jit(solution)/shard_map/reduce_second/ppermute | solution.py:880
  104.0 16.3 %collective-permute-start.23 = (bf16[320,768]{1,0:T(8,128)(2,1)S(1)}, bf16[320,768]{1,0:T(8,128)(2,1)S(1)}, u32[]{:S(2)}, u32[]{:S(2)}) collective-permute-start(bf16[320,768]{1,0:T(8,128)(2,1)S(1)} %get-tuple-element.187), channel_id=1, source_target_pairs={{0,0},{1,1},{2,4},{3,5},{4,2},{5,3},{6,6},{7,7},{8,8},{9,9},{10,12... | collective-permute-start | bytes 1474568 | tf_op jit(solution)/shard_map/out_move/ppermute | solution.py:880
  107.8 21.2 %collective-permute-start.29 = (bf16[2,4,240,384]{3,2,1,0:T(8,128)(2,1)S(1)}, bf16[2,4,240,384]{3,2,1,0:T(8,128)(2,1)S(1)}, u32[]{:S(2)}, u32[]{:S(2)}) collective-permute-start(bf16[2,4,240,384]{3,2,1,0:T(8,128)(2,1)S(1)} %get-tuple-element.200), channel_id=1, source_target_pairs={{0,8},{1,9},{2,10},{3,11},{4,20},{5,21},{6,22},{7,23},{8,0},{9,1},... | collective-permute-start | bytes 4423688 | tf_op jit(solution)/shard_map/expand_first/ppermute | solution.py:880
  131.1 24.3 %collective-permute-start.31 = (bf16[4,240,384]{2,1,0:T(8,128)(2,1)S(1)}, bf16[4,240,384]{2,1,0:T(8,128)(2,1)S(1)}, u32[]{:S(2)}, u32[]{:S(2)}) collective-permute-start(bf16[4,240,384]{2,1,0:T(8,128)(2,1)S(1)} %fusion), channel_id=1, source_target_pairs={{0,16},{1,17},{2,18},{3,19},{4,12},{5,13},{6,14},{7,15},{8,24},{9,... | collective-permute-start | bytes 2211848 | tf_op jit(solution)/shard_map/expand_second/ppermute | solution.py:880
  132.5 22.9 %collective-permute-start.30 = (bf16[368,768]{1,0:T(8,128)(2,1)S(1)}, bf16[368,768]{1,0:T(8,128)(2,1)S(1)}, u32[]{:S(2)}, u32[]{:S(2)}) collective-permute-start(bf16[368,768]{1,0:T(8,128)(2,1)S(1)} %get-tuple-element.202.sent_ref), channel_id=1, source_target_pairs={{0,1},{1,0},{2,3},{3,2},{4,5},{5,4},{6,7},{7,6},{8,9},{9,8},{10,11... | collective-permute-start | bytes 1695752 | tf_op jit(solution)/shard_map/near_pair/ppermute | solution.py:880
  132.9 16.0 %collective-permute-start.24 = (bf16[144,768]{1,0:T(8,128)(2,1)S(1)}, bf16[144,768]{1,0:T(8,128)(2,1)S(1)}, u32[]{:S(2)}, u32[]{:S(2)}) collective-permute-start(bf16[144,768]{1,0:T(8,128)(2,1)S(1)} %get-tuple-element.194), channel_id=1, source_target_pairs={{0,8},{1,9},{2,10},{3,11},{4,12},{5,13},{6,14},{7,15},{8,0},{9,1},... | collective-permute-start | bytes 663560 | tf_op jit(solution)/shard_map/triple_x/ppermute | solution.py:880
  133.8 15.0 %collective-permute-start.25 = (bf16[144,768]{1,0:T(8,128)(2,1)S(1)}, bf16[144,768]{1,0:T(8,128)(2,1)S(1)}, u32[]{:S(2)}, u32[]{:S(2)}) collective-permute-start(bf16[144,768]{1,0:T(8,128)(2,1)S(1)} %get-tuple-element.195), channel_id=1, source_target_pairs={{0,16},{1,17},{2,18},{3,19},{4,20},{5,21},{6,22},{7,23},{8,24},{9,... | collective-permute-start | bytes 663560 | tf_op jit(solution)/shard_map/triple_y/ppermute | solution.py:880
  134.5 16.8 %collective-permute-start.26 = (bf16[144,768]{1,0:T(8,128)(2,1)S(1)}, bf16[144,768]{1,0:T(8,128)(2,1)S(1)}, u32[]{:S(2)}, u32[]{:S(2)}) collective-permute-start(bf16[144,768]{1,0:T(8,128)(2,1)S(1)} %get-tuple-element.196), channel_id=1, source_target_pairs={{0,24},{1,25},{2,26},{3,27},{4,28},{5,29},{6,30},{7,31},{8,16},{9,... | collective-permute-start | bytes 663560 | tf_op jit(solution)/shard_map/triple_xy/ppermute | solution.py:880
  155.6 10.9 %collective-permute-start.34 = (bf16[2,240,384]{2,1,0:T(8,128)(2,1)S(1)}, bf16[2,240,384]{2,1,0:T(8,128)(2,1)S(1)}, u32[]{:S(2)}, u32[]{:S(2)}) collective-permute-start(bf16[2,240,384]{2,1,0:T(8,128)(2,1)S(1)} %get-tuple-element.244), channel_id=1, source_target_pairs={{0,1},{1,0},{2,3},{3,2},{4,5},{5,4},{6,7},{7,6},{8,9},{9,8},{10,11... | collective-permute-start | bytes 1105928 | tf_op jit(solution)/shard_map/expand_pair/ppermute | solution.py:880
  156.4 8.6 %collective-permute-start.33 = (bf16[192,768]{1,0:T(8,128)(2,1)S(1)}, bf16[192,768]{1,0:T(8,128)(2,1)S(1)}, u32[]{:S(2)}, u32[]{:S(2)}) collective-permute-start(bf16[192,768]{1,0:T(8,128)(2,1)S(1)} %home_part.1.sent_ref), channel_id=1, source_target_pairs={{2,0},{3,1},{4,6},{5,7},{10,8},{11,9},{12,14},{13,15},{18,16},{19,... | collective-permute-start | bytes 884744 | tf_op jit(solution)/shard_map/triple_home/ppermute | solution.py:880
  160.5 16.6 %collective-permute-start.39 = (bf16[320,768]{1,0:T(8,128)(2,1)S(1)}, bf16[320,768]{1,0:T(8,128)(2,1)S(1)}, u32[]{:S(2)}, u32[]{:S(2)}) collective-permute-start(bf16[320,768]{1,0:T(8,128)(2,1)S(1)} %front_part.1), channel_id=1, source_target_pairs={{0,0},{1,1},{2,4},{3,5},{4,2},{5,3},{6,6},{7,7},{8,8},{9,9},{10,12... | collective-permute-start | bytes 1474568 | tf_op jit(solution)/shard_map/rows_home/ppermute | solution.py:880
  167.2 14.1 %collective-permute-start.37 = (bf16[192,768]{1,0:T(8,128)(2,1)S(1)}, bf16[192,768]{1,0:T(8,128)(2,1)S(1)}, u32[]{:S(2)}, u32[]{:S(2)}) collective-permute-start(bf16[192,768]{1,0:T(8,128)(2,1)S(1)} %spread_part.1.s0_ref), channel_id=1, source_target_pairs={{0,24},{1,25},{6,30},{7,31},{8,16},{9,17},{14,22},{15,23},{16,8},{... | collective-permute-start | bytes 884744 | tf_op jit(solution)/shard_map/triple_spread/ppermute | solution.py:880
  167.8 13.4 %collective-permute-start.36 = (bf16[192,768]{1,0:T(8,128)(2,1)S(1)}, bf16[192,768]{1,0:T(8,128)(2,1)S(1)}, u32[]{:S(2)}, u32[]{:S(2)}) collective-permute-start(bf16[192,768]{1,0:T(8,128)(2,1)S(1)} %spread_part.1.s0_ref), channel_id=1, source_target_pairs={{0,16},{1,17},{6,22},{7,23},{8,24},{9,25},{14,30},{15,31},{16,0},{... | collective-permute-start | bytes 884744 | tf_op jit(solution)/shard_map/triple_spread/ppermute | solution.py:880
  168.5 12.8 %collective-permute-start.35 = (bf16[192,768]{1,0:T(8,128)(2,1)S(1)}, bf16[192,768]{1,0:T(8,128)(2,1)S(1)}, u32[]{:S(2)}, u32[]{:S(2)}) collective-permute-start(bf16[192,768]{1,0:T(8,128)(2,1)S(1)} %spread_part.1.s0_ref), channel_id=1, source_target_pairs={{0,8},{1,9},{6,14},{7,15},{8,0},{9,1},{14,6},{15,7},{16,24},{17,25... | collective-permute-start | bytes 884744 | tf_op jit(solution)/shard_map/triple_spread/ppermute | solution.py:880
  169.3 12.0 %collective-permute-start.38 = (bf16[240,384]{1,0:T(8,128)(2,1)S(1)}, bf16[240,384]{1,0:T(8,128)(2,1)S(1)}, u32[]{:S(2)}, u32[]{:S(2)}) collective-permute-start(bf16[240,384]{1,0:T(8,128)(2,1)S(1)} %fusion.6), channel_id=1, source_target_pairs={{0,2},{1,3},{2,0},{3,1},{4,6},{5,7},{6,4},{7,5},{8,10},{9,11},{10,... | collective-permute-start | bytes 552968 | tf_op jit(solution)/shard_map/expand_across/ppermute | solution.py:880
  182.0 8.0 %collective-permute-start.40 = (bf16[672,768]{1,0:T(8,128)(2,1)S(1)}, bf16[672,768]{1,0:T(8,128)(2,1)S(1)}, u32[]{:S(2)}, u32[]{:S(2)}) collective-permute-start(bf16[672,768]{1,0:T(8,128)(2,1)S(1)} %get-tuple-element.218.sent_ref), channel_id=1, source_target_pairs={{0,4},{1,5},{2,6},{3,7},{4,0},{5,1},{6,2},{7,3},{8,12},{9,13},{10,... | collective-permute-start | bytes 3096584 | tf_op jit(solution)/shard_map/last_core/ppermute | solution.py:880
  (32 other events, 182.9 us)
